TPU v7x, 32 devices: a whole 2x2x4 slice. The times are simulated.
32 devices in a mesh: ctx: 32 (over z, y, x, core), chan: 1.
Axes of the slice: x: 2, y: 2, z: 4, core: 2. Of those that a mesh axis runs over, the one named last changes fastest.
Arguments:
- features: bfloat16 [8192, 3, 8192], P('ctx', None, 'chan'), may hold values from -29 to 29
- short_taps: float32 [3, 3, 8192], P(None, None, 'chan'), may hold values from -3 to 3
- decay_rate: float32 [16, 8192], P(None, 'chan'), may hold values from 6.1035156e-05 to 0.0333333333
- residue: float32 [16, 8192], P(None, 'chan'), may hold values from -1.5 to 1.5
- skip_gain: float32 [8192], P('chan'), may hold values from -4 to 4
- norm_gain: float32 [8192], P('chan'), may hold values from 0.5 to 1.5
- contig_lengths: int32 [4], replicated, may hold values from 1 to 4096, 8192 in all
Outputs:
- normed: bfloat16 [8192, 8192], P('ctx', 'chan')
Inputs may be any that keep to these rules, and one draw needn't show every extreme that they name: `contig_lengths`: the lengths sum to 8192 and the longest is exactly 4096.
All inputs are finite; a program needn't handle non-finite values.
Results may differ from a plain program's by a relative error of at most 0.0024.
Values may be sent and summed in bfloat16 or wider, within the bound.
A program may use at most 128 MiB of HBM per device.

v0:
```python
import jax
import jax.numpy as jnp
from jax import lax
from jax.sharding import PartitionSpec as P

D = 8192


eps_norm = 1e-05


def passed_along(value, axis, by):
    count = lax.axis_size(axis)
    pairs = [(i, i + by) for i in range(count) if 0 <= i + by < count]
    return lax.ppermute(value, axis, pairs)


def carried_in(value, axis, join, neutral):
    count, mine = (lax.axis_size(axis), lax.axis_index(axis))
    pieces = jax.tree.map(lambda part: lax.all_gather(part, axis), value)
    subtotal = jax.tree.map(
        lambda part, zero: jnp.full_like(part, 0) + jnp.asarray(zero, part.dtype), value, neutral
    )

    def turn(position, subtotal):
        longer = join(subtotal, jax.tree.map(lambda part: part[position], pieces))
        return jax.tree.map(lambda new, old: jnp.where(position < mine, new, old), longer, subtotal)

    return lax.fori_loop(0, count - 1, turn, subtotal)


def segment_of(places, bounds):
    return jnp.sum((places[:, None] >= bounds[None, :]).astype(jnp.int32), axis=1)


def shards(features, short_taps, decay_rate, residue, skip_gain, norm_gain, contig_lengths):
    tok_rows = features.shape[0]
    channels = features.shape[2]
    poles = decay_rate.shape[0]
    anchor = lax.axis_index("ctx") * tok_rows
    bounds = jnp.cumsum(contig_lengths)[:-1]
    places = anchor + jnp.arange(tok_rows, dtype=jnp.int32)
    segment = segment_of(places, bounds)
    keep_one = ((segment_of(places - 1, bounds) == segment) & (places >= 1)).astype(jnp.float32)
    keep_two = ((segment_of(places - 2, bounds) == segment) & (places >= 2)).astype(jnp.float32)
    before = segment_of(jnp.reshape(anchor - 1, (1,)), bounds)[0]
    joined = ((segment == before) & (anchor >= 1)).astype(jnp.float32)
    edge_rows = passed_along(features[tok_rows - 2 :], "ctx", 1)
    extended = jnp.concatenate([edge_rows, features], axis=0).astype(jnp.float32)
    mixed_rows = (
        short_taps[0] * extended[2:]
        + short_taps[1] * extended[1:-1] * keep_one[:, None, None]
        + short_taps[2] * extended[:-2] * keep_two[:, None, None]
    )
    query_part = mixed_rows[:, 0]
    product = mixed_rows[:, 1] * mixed_rows[:, 2]
    input_scale = jnp.sqrt(1.0 - jnp.exp(-2.0 * decay_rate))
    block_rows = min(tok_rows, 128)
    steps_in = jnp.arange(block_rows, dtype=jnp.float32)
    carries = jnp.zeros((poles, channels), jnp.float32)
    pieces = []
    for block_index in range(tok_rows // block_rows):
        first_row = block_index * block_rows
        seg_block = segment[first_row : first_row + block_rows]
        lower_mask = (
            (steps_in[None, :] <= steps_in[:, None]) & (seg_block[:, None] == seg_block[None, :])
        ).astype(jnp.float32)
        if first_row > 0:
            head_block = (seg_block == segment[first_row - 1]).astype(jnp.float32)
        else:
            head_block = jnp.zeros((block_rows,), jnp.float32)
        drive_rows = product[first_row : first_row + block_rows]

        def one_mode(mode_index, carry):
            total_rows, states = carry
            rate_row = decay_rate[mode_index]
            scaled = jnp.exp(rate_row[None, :] * steps_in[:, None]) * (
                drive_rows * input_scale[mode_index][None, :]
            )
            summed = jnp.dot(
                lower_mask,
                scaled,
                precision=lax.Precision.HIGHEST,
                preferred_element_type=jnp.float32,
            )
            state_rows = (
                jnp.exp(-rate_row[None, :] * steps_in[:, None]) * summed
                + jnp.exp(-rate_row[None, :] * (steps_in[:, None] + 1.0))
                * states[mode_index][None, :]
                * head_block[:, None]
            )
            total_rows = total_rows + residue[mode_index][None, :] * state_rows
            states = states.at[mode_index].set(state_rows[block_rows - 1])
            return (total_rows, states)

        block_sum, carries = lax.fori_loop(
            0, poles, one_mode, (jnp.zeros((block_rows, channels), jnp.float32), carries)
        )
        pieces.append(block_sum)
    local_filtered = jnp.concatenate(pieces, axis=0)
    through = jnp.exp(-decay_rate * tok_rows) * joined[tok_rows - 1]

    def chain_factor(earlier, later):
        return (earlier[0] * later[0], later[0] * earlier[1] + later[1])

    arrived = carried_in(
        (through, carries), "ctx", chain_factor, (jnp.ones_like(through), jnp.zeros_like(carries))
    )[1]
    offsets = jnp.arange(tok_rows, dtype=jnp.float32) + 1.0
    weight_in = residue * arrived
    incoming = (
        jnp.sum(
            jnp.exp(-decay_rate[None, :, :] * offsets[:, None, None]) * weight_in[None, :, :],
            axis=1,
        )
        * joined[:, None]
    )
    response = query_part * (local_filtered + incoming + skip_gain[None, :] * product)
    squares = lax.psum(jnp.sum(response * response, axis=1), "chan")
    scale_rows = lax.rsqrt(squares / D + eps_norm)
    return (response * scale_rows[:, None] * norm_gain[None, :]).astype(jnp.bfloat16)


def solution(mesh):
    placed = (
        P("ctx", None, "chan"),
        P(None, None, "chan"),
        P(None, "chan"),
        P(None, "chan"),
        P("chan"),
        P("chan"),
        P(),
    )
    return jax.shard_map(
        shards, mesh=mesh, in_specs=placed, out_specs=P("ctx", "chan"), check_vma=False
    )
```

profile of v0, /device:TPU:0, one launch (start us, length us, event | category | flops | bytes accessed | tf_op | source)
XLA Modules:
  0.0 789.6 jit_solution(8542413304742055795)
XLA Ops:
  7.6 2.4 collective-permute-start
  12.8 2.8 fusion.51
  18.0 14.8 %maximum_convert_fusion = f32[258,3,8192]{2,0,1:T(8,128)} fusion(bf16[256,3,8192]{2,0,1:T(8,128)(2,1)} %param.17, bf16[2,3,8192]{2,0,1:T(2,128)(2,1)S(1)} %collective-permute-done), kind=kLoop, calls=%fused_computation.65 | loop fusion | flops 25362432 | bytes 38043648 | tf_op jit(solution)/shard_map/convert_element_type | solution.py:49
  32.9 35.0 %fusion.40 = f32[256,3,8192]{2,0,1:T(8,128)} fusion(f32[258,3,8192]{2,0,1:T(8,128)} %maximum_convert_fusion, f32[256]{0:T(256)S(1)} %get-tuple-element.692, f32[3,8192]{1,0:T(4,128)S(1)} %get-tuple-element.687, f32[256]{0:T(256)S(1)} %get-tuple-element.693, f32[3,8192]{1,0:T(4,128)S(1)} %get-tuple-element.688, f32[3,8192]{1,0:T(4,128)S(1)} %get-tuple-element.686), kind=kLoop, calls=%fused_computation.60 | loop fusion | flops 44040192 | bytes 100960256 | tf_op jit(solution)/shard_map/add | solution.py:51
  67.9 10.3 %slice_multiply_fusion.3 = f32[256,1,8192]{2,0,1:T(8,128)} fusion(f32[256,3,8192]{2,0,1:T(8,128)} %fusion.40), kind=kLoop, calls=%fused_computation.66 | loop fusion | flops 2097152 | bytes 25165824 | tf_op jit(solution)/shard_map/mul | solution.py:56
  78.2 9.4 %slice_bitcast_fusion.1 = (f32[128,8192]{1,0:T(8,128)}, f32[128,8192]{1,0:T(8,128)}) fusion(f32[256,1,8192]{2,0,1:T(8,128)} %slice_multiply_fusion.3), kind=kLoop, calls=%fused_computation.74 | loop fusion | bytes 16777216 | tf_op jit(solution)/shard_map/slice | solution.py:72
  87.7 229.0 %while.51 = (s32[]{:T(128)}, f32[128,8192]{1,0:T(8,128)}, f32[16,8192]{1,0:T(8,128)S(1)}, f32[16,8192]{1,0:T(8,128)S(1)}, f32[16,8192]{1,0:T(8,128)}, /*index=5*...) while((s32[]{:T(128)}, f32[128,8192]{1,0:T(8,128)}, ...), condition=%wide.region_6.7_spmd.clone.clone, body=%wide.region_4.6_spmd.clone.clone.sunk | while | flops 1623277696 | bytes 17401496 | solution.py:96
  88.8 10.4 %select_add_fusion.4 = (f32[128,8192]{1,0:T(8,128)}, f32[128,8192]{1,0:T(8,128)S(1)}) fusion(f32[128,8192]{1,0:T(8,128)} %get-tuple-element.874, f32[8192]{0:T(1024)S(1)} %bitcast.91, pred[]{:T(512)S(6)} %compare.62, f32[8192]{0:T(1024)S(1)} %bitcast.87, f32[128]{0:T(128)S(1)} %iota_add_fusion.6, s32[128]{0:T(128)S(1)} %get-tuple-element.892, ...), kind=kOutput, calls=%fused_computation.15.clone.1 | convolution fusion | flops 1623261184 | bytes 16942080 | tf_op jit(solution)/shard_map/while/body/eval_jaxpr/dot_general | solution.py:80
  101.9 11.7 %select_add_fusion.4 = (f32[128,8192]{1,0:T(8,128)}, f32[128,8192]{1,0:T(8,128)S(1)}) fusion(f32[128,8192]{1,0:T(8,128)} %get-tuple-element.874, f32[8192]{0:T(1024)S(1)} %bitcast.91, pred[]{:T(512)S(6)} %compare.62, f32[8192]{0:T(1024)S(1)} %bitcast.87, f32[128]{0:T(128)S(1)} %iota_add_fusion.6, s32[128]{0:T(128)S(1)} %get-tuple-element.892, ...), kind=kOutput, calls=%fused_computation.15.clone.1 | convolution fusion | flops 1623261184 | bytes 16942080 | tf_op jit(solution)/shard_map/while/body/eval_jaxpr/dot_general | solution.py:80
  116.3 11.7 %select_add_fusion.4 = (f32[128,8192]{1,0:T(8,128)}, f32[128,8192]{1,0:T(8,128)S(1)}) fusion(f32[128,8192]{1,0:T(8,128)} %get-tuple-element.874, f32[8192]{0:T(1024)S(1)} %bitcast.91, pred[]{:T(512)S(6)} %compare.62, f32[8192]{0:T(1024)S(1)} %bitcast.87, f32[128]{0:T(128)S(1)} %iota_add_fusion.6, s32[128]{0:T(128)S(1)} %get-tuple-element.892, ...), kind=kOutput, calls=%fused_computation.15.clone.1 | convolution fusion | flops 1623261184 | bytes 16942080 | tf_op jit(solution)/shard_map/while/body/eval_jaxpr/dot_general | solution.py:80
  130.7 12.0 %select_add_fusion.4 = (f32[128,8192]{1,0:T(8,128)}, f32[128,8192]{1,0:T(8,128)S(1)}) fusion(f32[128,8192]{1,0:T(8,128)} %get-tuple-element.874, f32[8192]{0:T(1024)S(1)} %bitcast.91, pred[]{:T(512)S(6)} %compare.62, f32[8192]{0:T(1024)S(1)} %bitcast.87, f32[128]{0:T(128)S(1)} %iota_add_fusion.6, s32[128]{0:T(128)S(1)} %get-tuple-element.892, ...), kind=kOutput, calls=%fused_computation.15.clone.1 | convolution fusion | flops 1623261184 | bytes 16942080 | tf_op jit(solution)/shard_map/while/body/eval_jaxpr/dot_general | solution.py:80
  145.3 11.7 %select_add_fusion.4 = (f32[128,8192]{1,0:T(8,128)}, f32[128,8192]{1,0:T(8,128)S(1)}) fusion(f32[128,8192]{1,0:T(8,128)} %get-tuple-element.874, f32[8192]{0:T(1024)S(1)} %bitcast.91, pred[]{:T(512)S(6)} %compare.62, f32[8192]{0:T(1024)S(1)} %bitcast.87, f32[128]{0:T(128)S(1)} %iota_add_fusion.6, s32[128]{0:T(128)S(1)} %get-tuple-element.892, ...), kind=kOutput, calls=%fused_computation.15.clone.1 | convolution fusion | flops 1623261184 | bytes 16942080 | tf_op jit(solution)/shard_map/while/body/eval_jaxpr/dot_general | solution.py:80
  159.7 11.7 %select_add_fusion.4 = (f32[128,8192]{1,0:T(8,128)}, f32[128,8192]{1,0:T(8,128)S(1)}) fusion(f32[128,8192]{1,0:T(8,128)} %get-tuple-element.874, f32[8192]{0:T(1024)S(1)} %bitcast.91, pred[]{:T(512)S(6)} %compare.62, f32[8192]{0:T(1024)S(1)} %bitcast.87, f32[128]{0:T(128)S(1)} %iota_add_fusion.6, s32[128]{0:T(128)S(1)} %get-tuple-element.892, ...), kind=kOutput, calls=%fused_computation.15.clone.1 | convolution fusion | flops 1623261184 | bytes 16942080 | tf_op jit(solution)/shard_map/while/body/eval_jaxpr/dot_general | solution.py:80
  174.1 11.7 %select_add_fusion.4 = (f32[128,8192]{1,0:T(8,128)}, f32[128,8192]{1,0:T(8,128)S(1)}) fusion(f32[128,8192]{1,0:T(8,128)} %get-tuple-element.874, f32[8192]{0:T(1024)S(1)} %bitcast.91, pred[]{:T(512)S(6)} %compare.62, f32[8192]{0:T(1024)S(1)} %bitcast.87, f32[128]{0:T(128)S(1)} %iota_add_fusion.6, s32[128]{0:T(128)S(1)} %get-tuple-element.892, ...), kind=kOutput, calls=%fused_computation.15.clone.1 | convolution fusion | flops 1623261184 | bytes 16942080 | tf_op jit(solution)/shard_map/while/body/eval_jaxpr/dot_general | solution.py:80
  188.4 11.7 %select_add_fusion.4 = (f32[128,8192]{1,0:T(8,128)}, f32[128,8192]{1,0:T(8,128)S(1)}) fusion(f32[128,8192]{1,0:T(8,128)} %get-tuple-element.874, f32[8192]{0:T(1024)S(1)} %bitcast.91, pred[]{:T(512)S(6)} %compare.62, f32[8192]{0:T(1024)S(1)} %bitcast.87, f32[128]{0:T(128)S(1)} %iota_add_fusion.6, s32[128]{0:T(128)S(1)} %get-tuple-element.892, ...), kind=kOutput, calls=%fused_computation.15.clone.1 | convolution fusion | flops 1623261184 | bytes 16942080 | tf_op jit(solution)/shard_map/while/body/eval_jaxpr/dot_general | solution.py:80
  202.8 11.7 %select_add_fusion.4 = (f32[128,8192]{1,0:T(8,128)}, f32[128,8192]{1,0:T(8,128)S(1)}) fusion(f32[128,8192]{1,0:T(8,128)} %get-tuple-element.874, f32[8192]{0:T(1024)S(1)} %bitcast.91, pred[]{:T(512)S(6)} %compare.62, f32[8192]{0:T(1024)S(1)} %bitcast.87, f32[128]{0:T(128)S(1)} %iota_add_fusion.6, s32[128]{0:T(128)S(1)} %get-tuple-element.892, ...), kind=kOutput, calls=%fused_computation.15.clone.1 | convolution fusion | flops 1623261184 | bytes 16942080 | tf_op jit(solution)/shard_map/while/body/eval_jaxpr/dot_general | solution.py:80
  217.2 11.7 %select_add_fusion.4 = (f32[128,8192]{1,0:T(8,128)}, f32[128,8192]{1,0:T(8,128)S(1)}) fusion(f32[128,8192]{1,0:T(8,128)} %get-tuple-element.874, f32[8192]{0:T(1024)S(1)} %bitcast.91, pred[]{:T(512)S(6)} %compare.62, f32[8192]{0:T(1024)S(1)} %bitcast.87, f32[128]{0:T(128)S(1)} %iota_add_fusion.6, s32[128]{0:T(128)S(1)} %get-tuple-element.892, ...), kind=kOutput, calls=%fused_computation.15.clone.1 | convolution fusion | flops 1623261184 | bytes 16942080 | tf_op jit(solution)/shard_map/while/body/eval_jaxpr/dot_general | solution.py:80
  231.6 11.7 %select_add_fusion.4 = (f32[128,8192]{1,0:T(8,128)}, f32[128,8192]{1,0:T(8,128)S(1)}) fusion(f32[128,8192]{1,0:T(8,128)} %get-tuple-element.874, f32[8192]{0:T(1024)S(1)} %bitcast.91, pred[]{:T(512)S(6)} %compare.62, f32[8192]{0:T(1024)S(1)} %bitcast.87, f32[128]{0:T(128)S(1)} %iota_add_fusion.6, s32[128]{0:T(128)S(1)} %get-tuple-element.892, ...), kind=kOutput, calls=%fused_computation.15.clone.1 | convolution fusion | flops 1623261184 | bytes 16942080 | tf_op jit(solution)/shard_map/while/body/eval_jaxpr/dot_general | solution.py:80
  245.9 11.7 %select_add_fusion.4 = (f32[128,8192]{1,0:T(8,128)}, f32[128,8192]{1,0:T(8,128)S(1)}) fusion(f32[128,8192]{1,0:T(8,128)} %get-tuple-element.874, f32[8192]{0:T(1024)S(1)} %bitcast.91, pred[]{:T(512)S(6)} %compare.62, f32[8192]{0:T(1024)S(1)} %bitcast.87, f32[128]{0:T(128)S(1)} %iota_add_fusion.6, s32[128]{0:T(128)S(1)} %get-tuple-element.892, ...), kind=kOutput, calls=%fused_computation.15.clone.1 | convolution fusion | flops 1623261184 | bytes 16942080 | tf_op jit(solution)/shard_map/while/body/eval_jaxpr/dot_general | solution.py:80
  260.3 11.7 %select_add_fusion.4 = (f32[128,8192]{1,0:T(8,128)}, f32[128,8192]{1,0:T(8,128)S(1)}) fusion(f32[128,8192]{1,0:T(8,128)} %get-tuple-element.874, f32[8192]{0:T(1024)S(1)} %bitcast.91, pred[]{:T(512)S(6)} %compare.62, f32[8192]{0:T(1024)S(1)} %bitcast.87, f32[128]{0:T(128)S(1)} %iota_add_fusion.6, s32[128]{0:T(128)S(1)} %get-tuple-element.892, ...), kind=kOutput, calls=%fused_computation.15.clone.1 | convolution fusion | flops 1623261184 | bytes 16942080 | tf_op jit(solution)/shard_map/while/body/eval_jaxpr/dot_general | solution.py:80
  274.7 11.7 %select_add_fusion.4 = (f32[128,8192]{1,0:T(8,128)}, f32[128,8192]{1,0:T(8,128)S(1)}) fusion(f32[128,8192]{1,0:T(8,128)} %get-tuple-element.874, f32[8192]{0:T(1024)S(1)} %bitcast.91, pred[]{:T(512)S(6)} %compare.62, f32[8192]{0:T(1024)S(1)} %bitcast.87, f32[128]{0:T(128)S(1)} %iota_add_fusion.6, s32[128]{0:T(128)S(1)} %get-tuple-element.892, ...), kind=kOutput, calls=%fused_computation.15.clone.1 | convolution fusion | flops 1623261184 | bytes 16942080 | tf_op jit(solution)/shard_map/while/body/eval_jaxpr/dot_general | solution.py:80
  289.1 11.7 %select_add_fusion.4 = (f32[128,8192]{1,0:T(8,128)}, f32[128,8192]{1,0:T(8,128)S(1)}) fusion(f32[128,8192]{1,0:T(8,128)} %get-tuple-element.874, f32[8192]{0:T(1024)S(1)} %bitcast.91, pred[]{:T(512)S(6)} %compare.62, f32[8192]{0:T(1024)S(1)} %bitcast.87, f32[128]{0:T(128)S(1)} %iota_add_fusion.6, s32[128]{0:T(128)S(1)} %get-tuple-element.892, ...), kind=kOutput, calls=%fused_computation.15.clone.1 | convolution fusion | flops 1623261184 | bytes 16942080 | tf_op jit(solution)/shard_map/while/body/eval_jaxpr/dot_general | solution.py:80
  303.4 11.7 %select_add_fusion.4 = (f32[128,8192]{1,0:T(8,128)}, f32[128,8192]{1,0:T(8,128)S(1)}) fusion(f32[128,8192]{1,0:T(8,128)} %get-tuple-element.874, f32[8192]{0:T(1024)S(1)} %bitcast.91, pred[]{:T(512)S(6)} %compare.62, f32[8192]{0:T(1024)S(1)} %bitcast.87, f32[128]{0:T(128)S(1)} %iota_add_fusion.6, s32[128]{0:T(128)S(1)} %get-tuple-element.892, ...), kind=kOutput, calls=%fused_computation.15.clone.1 | convolution fusion | flops 1623261184 | bytes 16942080 | tf_op jit(solution)/shard_map/while/body/eval_jaxpr/dot_general | solution.py:80
  316.7 229.4 %while.52 = (s32[]{:T(128)}, f32[128,8192]{1,0:T(8,128)}, f32[16,8192]{1,0:T(8,128)S(1)}, f32[16,8192]{1,0:T(8,128)S(1)}, f32[16,8192]{1,0:T(8,128)}, /*index=5*...) while((s32[]{:T(128)}, f32[128,8192]{1,0:T(8,128)}, ...), condition=%wide.region_9.10_spmd.clone.clone, body=%wide.region_7.9_spmd.clone.clone.sunk | while | flops 1623277696 | bytes 17402016 | solution.py:96
  318.0 10.5 %select_add_fusion.5 = (f32[128,8192]{1,0:T(8,128)}, f32[128,8192]{1,0:T(8,128)S(1)}) fusion(f32[128,8192]{1,0:T(8,128)} %get-tuple-element.911, f32[8192]{0:T(1024)S(1)} %bitcast.94, pred[]{:T(512)S(6)} %compare.65, f32[128]{0:T(128)S(1)} %get-tuple-element.930, f32[8192]{0:T(1024)S(1)} %bitcast.88, f32[128]{0:T(128)S(1)} %iota_add_fusion.7, ...), kind=kOutput, calls=%fused_computation.40.clone.1 | convolution fusion | flops 1623261184 | bytes 16942592 | tf_op jit(solution)/shard_map/while/body/eval_jaxpr/dot_general | solution.py:80
  331.1 11.7 %select_add_fusion.5 = (f32[128,8192]{1,0:T(8,128)}, f32[128,8192]{1,0:T(8,128)S(1)}) fusion(f32[128,8192]{1,0:T(8,128)} %get-tuple-element.911, f32[8192]{0:T(1024)S(1)} %bitcast.94, pred[]{:T(512)S(6)} %compare.65, f32[128]{0:T(128)S(1)} %get-tuple-element.930, f32[8192]{0:T(1024)S(1)} %bitcast.88, f32[128]{0:T(128)S(1)} %iota_add_fusion.7, ...), kind=kOutput, calls=%fused_computation.40.clone.1 | convolution fusion | flops 1623261184 | bytes 16942592 | tf_op jit(solution)/shard_map/while/body/eval_jaxpr/dot_general | solution.py:80
  345.5 11.7 %select_add_fusion.5 = (f32[128,8192]{1,0:T(8,128)}, f32[128,8192]{1,0:T(8,128)S(1)}) fusion(f32[128,8192]{1,0:T(8,128)} %get-tuple-element.911, f32[8192]{0:T(1024)S(1)} %bitcast.94, pred[]{:T(512)S(6)} %compare.65, f32[128]{0:T(128)S(1)} %get-tuple-element.930, f32[8192]{0:T(1024)S(1)} %bitcast.88, f32[128]{0:T(128)S(1)} %iota_add_fusion.7, ...), kind=kOutput, calls=%fused_computation.40.clone.1 | convolution fusion | flops 1623261184 | bytes 16942592 | tf_op jit(solution)/shard_map/while/body/eval_jaxpr/dot_general | solution.py:80
  359.9 11.7 %select_add_fusion.5 = (f32[128,8192]{1,0:T(8,128)}, f32[128,8192]{1,0:T(8,128)S(1)}) fusion(f32[128,8192]{1,0:T(8,128)} %get-tuple-element.911, f32[8192]{0:T(1024)S(1)} %bitcast.94, pred[]{:T(512)S(6)} %compare.65, f32[128]{0:T(128)S(1)} %get-tuple-element.930, f32[8192]{0:T(1024)S(1)} %bitcast.88, f32[128]{0:T(128)S(1)} %iota_add_fusion.7, ...), kind=kOutput, calls=%fused_computation.40.clone.1 | convolution fusion | flops 1623261184 | bytes 16942592 | tf_op jit(solution)/shard_map/while/body/eval_jaxpr/dot_general | solution.py:80
  374.3 11.7 %select_add_fusion.5 = (f32[128,8192]{1,0:T(8,128)}, f32[128,8192]{1,0:T(8,128)S(1)}) fusion(f32[128,8192]{1,0:T(8,128)} %get-tuple-element.911, f32[8192]{0:T(1024)S(1)} %bitcast.94, pred[]{:T(512)S(6)} %compare.65, f32[128]{0:T(128)S(1)} %get-tuple-element.930, f32[8192]{0:T(1024)S(1)} %bitcast.88, f32[128]{0:T(128)S(1)} %iota_add_fusion.7, ...), kind=kOutput, calls=%fused_computation.40.clone.1 | convolution fusion | flops 1623261184 | bytes 16942592 | tf_op jit(solution)/shard_map/while/body/eval_jaxpr/dot_general | solution.py:80
  388.7 11.7 %select_add_fusion.5 = (f32[128,8192]{1,0:T(8,128)}, f32[128,8192]{1,0:T(8,128)S(1)}) fusion(f32[128,8192]{1,0:T(8,128)} %get-tuple-element.911, f32[8192]{0:T(1024)S(1)} %bitcast.94, pred[]{:T(512)S(6)} %compare.65, f32[128]{0:T(128)S(1)} %get-tuple-element.930, f32[8192]{0:T(1024)S(1)} %bitcast.88, f32[128]{0:T(128)S(1)} %iota_add_fusion.7, ...), kind=kOutput, calls=%fused_computation.40.clone.1 | convolution fusion | flops 1623261184 | bytes 16942592 | tf_op jit(solution)/shard_map/while/body/eval_jaxpr/dot_general | solution.py:80
  403.2 11.7 %select_add_fusion.5 = (f32[128,8192]{1,0:T(8,128)}, f32[128,8192]{1,0:T(8,128)S(1)}) fusion(f32[128,8192]{1,0:T(8,128)} %get-tuple-element.911, f32[8192]{0:T(1024)S(1)} %bitcast.94, pred[]{:T(512)S(6)} %compare.65, f32[128]{0:T(128)S(1)} %get-tuple-element.930, f32[8192]{0:T(1024)S(1)} %bitcast.88, f32[128]{0:T(128)S(1)} %iota_add_fusion.7, ...), kind=kOutput, calls=%fused_computation.40.clone.1 | convolution fusion | flops 1623261184 | bytes 16942592 | tf_op jit(solution)/shard_map/while/body/eval_jaxpr/dot_general | solution.py:80
  417.6 11.7 %select_add_fusion.5 = (f32[128,8192]{1,0:T(8,128)}, f32[128,8192]{1,0:T(8,128)S(1)}) fusion(f32[128,8192]{1,0:T(8,128)} %get-tuple-element.911, f32[8192]{0:T(1024)S(1)} %bitcast.94, pred[]{:T(512)S(6)} %compare.65, f32[128]{0:T(128)S(1)} %get-tuple-element.930, f32[8192]{0:T(1024)S(1)} %bitcast.88, f32[128]{0:T(128)S(1)} %iota_add_fusion.7, ...), kind=kOutput, calls=%fused_computation.40.clone.1 | convolution fusion | flops 1623261184 | bytes 16942592 | tf_op jit(solution)/shard_map/while/body/eval_jaxpr/dot_general | solution.py:80
  432.0 11.7 %select_add_fusion.5 = (f32[128,8192]{1,0:T(8,128)}, f32[128,8192]{1,0:T(8,128)S(1)}) fusion(f32[128,8192]{1,0:T(8,128)} %get-tuple-element.911, f32[8192]{0:T(1024)S(1)} %bitcast.94, pred[]{:T(512)S(6)} %compare.65, f32[128]{0:T(128)S(1)} %get-tuple-element.930, f32[8192]{0:T(1024)S(1)} %bitcast.88, f32[128]{0:T(128)S(1)} %iota_add_fusion.7, ...), kind=kOutput, calls=%fused_computation.40.clone.1 | convolution fusion | flops 1623261184 | bytes 16942592 | tf_op jit(solution)/shard_map/while/body/eval_jaxpr/dot_general | solution.py:80
  446.4 11.7 %select_add_fusion.5 = (f32[128,8192]{1,0:T(8,128)}, f32[128,8192]{1,0:T(8,128)S(1)}) fusion(f32[128,8192]{1,0:T(8,128)} %get-tuple-element.911, f32[8192]{0:T(1024)S(1)} %bitcast.94, pred[]{:T(512)S(6)} %compare.65, f32[128]{0:T(128)S(1)} %get-tuple-element.930, f32[8192]{0:T(1024)S(1)} %bitcast.88, f32[128]{0:T(128)S(1)} %iota_add_fusion.7, ...), kind=kOutput, calls=%fused_computation.40.clone.1 | convolution fusion | flops 1623261184 | bytes 16942592 | tf_op jit(solution)/shard_map/while/body/eval_jaxpr/dot_general | solution.py:80
  460.8 11.7 %select_add_fusion.5 = (f32[128,8192]{1,0:T(8,128)}, f32[128,8192]{1,0:T(8,128)S(1)}) fusion(f32[128,8192]{1,0:T(8,128)} %get-tuple-element.911, f32[8192]{0:T(1024)S(1)} %bitcast.94, pred[]{:T(512)S(6)} %compare.65, f32[128]{0:T(128)S(1)} %get-tuple-element.930, f32[8192]{0:T(1024)S(1)} %bitcast.88, f32[128]{0:T(128)S(1)} %iota_add_fusion.7, ...), kind=kOutput, calls=%fused_computation.40.clone.1 | convolution fusion | flops 1623261184 | bytes 16942592 | tf_op jit(solution)/shard_map/while/body/eval_jaxpr/dot_general | solution.py:80
  475.2 11.7 %select_add_fusion.5 = (f32[128,8192]{1,0:T(8,128)}, f32[128,8192]{1,0:T(8,128)S(1)}) fusion(f32[128,8192]{1,0:T(8,128)} %get-tuple-element.911, f32[8192]{0:T(1024)S(1)} %bitcast.94, pred[]{:T(512)S(6)} %compare.65, f32[128]{0:T(128)S(1)} %get-tuple-element.930, f32[8192]{0:T(1024)S(1)} %bitcast.88, f32[128]{0:T(128)S(1)} %iota_add_fusion.7, ...), kind=kOutput, calls=%fused_computation.40.clone.1 | convolution fusion | flops 1623261184 | bytes 16942592 | tf_op jit(solution)/shard_map/while/body/eval_jaxpr/dot_general | solution.py:80
  489.6 11.7 %select_add_fusion.5 = (f32[128,8192]{1,0:T(8,128)}, f32[128,8192]{1,0:T(8,128)S(1)}) fusion(f32[128,8192]{1,0:T(8,128)} %get-tuple-element.911, f32[8192]{0:T(1024)S(1)} %bitcast.94, pred[]{:T(512)S(6)} %compare.65, f32[128]{0:T(128)S(1)} %get-tuple-element.930, f32[8192]{0:T(1024)S(1)} %bitcast.88, f32[128]{0:T(128)S(1)} %iota_add_fusion.7, ...), kind=kOutput, calls=%fused_computation.40.clone.1 | convolution fusion | flops 1623261184 | bytes 16942592 | tf_op jit(solution)/shard_map/while/body/eval_jaxpr/dot_general | solution.py:80
  504.0 11.7 %select_add_fusion.5 = (f32[128,8192]{1,0:T(8,128)}, f32[128,8192]{1,0:T(8,128)S(1)}) fusion(f32[128,8192]{1,0:T(8,128)} %get-tuple-element.911, f32[8192]{0:T(1024)S(1)} %bitcast.94, pred[]{:T(512)S(6)} %compare.65, f32[128]{0:T(128)S(1)} %get-tuple-element.930, f32[8192]{0:T(1024)S(1)} %bitcast.88, f32[128]{0:T(128)S(1)} %iota_add_fusion.7, ...), kind=kOutput, calls=%fused_computation.40.clone.1 | convolution fusion | flops 1623261184 | bytes 16942592 | tf_op jit(solution)/shard_map/while/body/eval_jaxpr/dot_general | solution.py:80
  518.4 11.7 %select_add_fusion.5 = (f32[128,8192]{1,0:T(8,128)}, f32[128,8192]{1,0:T(8,128)S(1)}) fusion(f32[128,8192]{1,0:T(8,128)} %get-tuple-element.911, f32[8192]{0:T(1024)S(1)} %bitcast.94, pred[]{:T(512)S(6)} %compare.65, f32[128]{0:T(128)S(1)} %get-tuple-element.930, f32[8192]{0:T(1024)S(1)} %bitcast.88, f32[128]{0:T(128)S(1)} %iota_add_fusion.7, ...), kind=kOutput, calls=%fused_computation.40.clone.1 | convolution fusion | flops 1623261184 | bytes 16942592 | tf_op jit(solution)/shard_map/while/body/eval_jaxpr/dot_general | solution.py:80
  532.8 11.7 %select_add_fusion.5 = (f32[128,8192]{1,0:T(8,128)}, f32[128,8192]{1,0:T(8,128)S(1)}) fusion(f32[128,8192]{1,0:T(8,128)} %get-tuple-element.911, f32[8192]{0:T(1024)S(1)} %bitcast.94, pred[]{:T(512)S(6)} %compare.65, f32[128]{0:T(128)S(1)} %get-tuple-element.930, f32[8192]{0:T(1024)S(1)} %bitcast.88, f32[128]{0:T(128)S(1)} %iota_add_fusion.7, ...), kind=kOutput, calls=%fused_computation.40.clone.1 | convolution fusion | flops 1623261184 | bytes 16942592 | tf_op jit(solution)/shard_map/while/body/eval_jaxpr/dot_general | solution.py:80
  547.0 117.4 %all-gather.7.cloned.1.call-done = f32[512,8192]{1,0:T(8,128)} async-done(((f32[16,8192]{1,0:T(8,128)}), f32[512,8192]{1,0:T(8,128)}) %all-gather.7.cloned.1.call-update) | async-done | bytes 16777232 | tf_op jit(solution)/shard_map/all_gather | solution.py:20
  664.4 52.0 %while.50 = (s32[]{:T(128)}, f32[16,8192]{1,0:T(8,128)S(1)}, s32[]{:T(128)}, f32[32,16,8192]{2,1,0:T(8,128)}, f32[32,16,8192]{2,1,0:T(8,128)}, /*index=5*/s32[]{:T(128)}, s32[]{:T(128)}) while((s32[]{:T(128)}, f32[16,8192]{1,0:T(8,128)S(1)}, s32[]{:T(128)}, f32[32,16,8192]{2,1,0:T(8,128)}, f32[32,16,8192]{2,1,0:T(8,128)}, ...), condition=%wide.region_12.13_spmd.clone, body=%wide.region_11.12_spmd.clone.sunk | while | flops 524292 | bytes 2097253 | solution.py:29
  666.1 1.7 fusion.56
  667.8 1.7 fusion.56
  669.4 1.7 fusion.56
  672.8 1.7 fusion.56
  674.5 1.7 fusion.56
  676.1 1.7 fusion.56
  677.8 1.7 fusion.56
  679.5 1.7 fusion.56
  681.2 1.7 fusion.56
  684.5 1.7 fusion.56
  686.2 1.7 fusion.56
  687.9 1.7 fusion.56
  691.2 1.7 fusion.56
  692.9 1.7 fusion.56
  694.6 1.7 fusion.56
  698.0 1.7 fusion.56
  699.6 1.7 fusion.56
  701.3 1.7 fusion.56
  704.7 1.7 fusion.56
  716.5 41.7 %multiply_reduce_fusion = f32[256,8192]{1,0:T(8,128)} fusion(f32[16,8192]{1,0:T(8,128)S(1)} %mul.547, f32[256]{0:T(256)S(1)} %iota_add_fusion.2, f32[16,8192]{1,0:T(8,128)S(1)} %get-tuple-element.683), kind=kLoop, calls=%fused_computation.57 | loop fusion | flops 98566144 | bytes 9438208 | tf_op jit(solution)/shard_map/reduce_sum | solution.py:112
  758.1 18.1 %multiply_reduce_fusion.1 = (f32[256]{0:T(256)S(1)}, f32[256,8192]{1,0:T(8,128)}) fusion(f32[8192]{0:T(1024)S(1)} %copy-done.4, f32[256,8192]{1,0:T(8,128)} %multiply_reduce_fusion, f32[256]{0:T(256)S(1)} %get-tuple-element.691, f32[128,8192]{1,0:T(8,128)} %get-tuple-element.482, f32[128,8192]{1,0:T(8,128)} %get-tuple-element.480, f32[256,3,8192]{2,0,1:T(8,128)} %fusion.40), kind=kLoop, calls=%fused_computation.73 | loop fusion | flops 18874112 | bytes 50366464 | tf_op jit(solution)/shard_map/reduce_sum | solution.py:119
  776.2 6.5 multiply_convert_fusion
  (239 shorter events, 111.1 us)
Async XLA Ops:
  6.5 540.5 %all-gather.5.cloned.1.call-start = ((), (), s32[]{:S(2)}) async-start(), calls=%async_computation | async-start | bytes 17301504 | tf_op jit(solution)/shard_map/all_gather | solution.py:20
  7.6 10.4 %collective-permute-start = (bf16[2,3,8192]{2,0,1:T(2,128)(2,1)S(1)}, bf16[2,3,8192]{2,0,1:T(2,128)(2,1)S(1)}, u32[]{:S(2)}, u32[]{:S(2)}) collective-permute-start(bf16[2,3,8192]{2,0,1:T(2,128)(2,1)S(1)} %slice.125), channel_id=1, source_target_pairs={{0,1},{1,2},{2,3},{3,4},{4,5},{5,6},{6,7},{7,8},{8,9},{9,10},{10,1... | collective-permute-start | bytes 294920 | tf_op jit(solution)/shard_map/ppermute | solution.py:15
  15.6 648.8 %all-gather.7.cloned.1.call-start = ((), (), s32[]{:S(2)}) async-start(), calls=%async_computation.1 | async-start | bytes 17301504 | tf_op jit(solution)/shard_map/all_gather | solution.py:20
  78.2 9.5 %copy-start.1 = (f32[16,8192]{1,0:T(8,128)S(1)}, f32[16,8192]{1,0:T(8,128)}, u32[]{:S(2)}) copy-start(f32[16,8192]{1,0:T(8,128)} %param.20) | copy-start | bytes 1572868
  78.2 9.5 %copy-start.2 = (s32[2]{0:T(128)S(1)}, s32[2]{0:T(128)}, u32[]{:S(2)}) copy-start(s32[2]{0:T(128)} %constant.181.clone.3) | copy-start | bytes 28
  546.1 0.8 copy-start
  716.5 41.7 %copy-start.4 = (f32[8192]{0:T(1024)S(1)}, f32[8192]{0:T(1024)}, u32[]{:S(2)}) copy-start(f32[8192]{0:T(1024)} %param.21) | copy-start | bytes 98308
  758.1 18.1 %copy-start.3 = (f32[8192]{0:T(1024)S(1)}, f32[8192]{0:T(1024)}, u32[]{:S(2)}) copy-start(f32[8192]{0:T(1024)} %param.22) | copy-start | bytes 98308
Sparse Core Ops, SparseCore 0:
  15.7 117.4 all-gather.4
  547.1 117.2 all-gather.6
where the time goes:
time: 792 us; the launch traced here: 790 us
  matrix products  373 us (47%)
  other arithmetic  261 us (33%)
  waiting for transfers between devices  117 us (15%)
  local copies, waits for them, and re-layouts  20.3 us (3%)
  between operations  13.6 us (2%)
    dot_general x32, matrix products, one_mode(): jnp.dot(lower_mask, scaled, precision=lax.Precision.HIGHEST, preferred_el...  373 us
    all_gather x2, waiting for transfers between devices, carried_in(): pieces = jax.tree.map(lambda part: lax.all_gather(part, axis), value)  117 us
    select_n x31, other arithmetic, turn(): jnp.where(position < mine, new, old)  51.3 us
    another operation x65, other arithmetic  45.2 us
    reduce_sum x1, other arithmetic, shards(): jnp.sum(jnp.exp(-decay_rate[None, :, :] * offsets[:, None, None]) * weigh...  41.7 us
    add x1, other arithmetic, shards(): short_taps[0] * extended[2:]  35 us
    neg x32, other arithmetic, one_mode(): -rate_row[None, :] * steps_in[:, None]  32.6 us
    reduce_sum x1, other arithmetic, shards(): squares = lax.psum(jnp.sum(response * response, axis=1), 'chan')  18.1 us
  transfers between devices with their start and end apart: 3, of which 1 were waited for; matrix products, arithmetic and copies ran while one was open for 68% of the time, Pallas kernels for 0%

commit v1 on v0

v1 whole, which is shorter than its diff:
```python
import functools

import jax
import jax.numpy as jnp
import numpy as np
from jax import lax
from jax.experimental import pallas as pl
from jax.experimental.pallas import tpu as pltpu
from jax.sharding import PartitionSpec as P

D = 8192
eps_norm = 1e-05
RATE_TOP = 1.0 / 30.0 * (1.0 + 1e-6)
BLOCK = 32
WIDE = 16
NEAR = 7
F32 = jnp.float32
BF16 = jnp.bfloat16


def nodes_of(count):
    angle = (2 * np.arange(count) + 1) * np.pi / (2 * count)
    return RATE_TOP / 2 * (1 - np.cos(angle))


def lagrange(rate, nodes):
    count = len(nodes)
    unit = nodes / RATE_TOP
    scaled = rate * F32(1.0 / RATE_TOP)
    gaps = [scaled - F32(u) for u in unit]
    ahead = [None] * count
    for i in range(1, count):
        ahead[i] = gaps[i - 1] if i == 1 else ahead[i - 1] * gaps[i - 1]
    weights = [None] * count
    after = None
    for i in reversed(range(count)):
        norm = F32(1.0 / np.prod([unit[i] - unit[j] for j in range(count) if j != i]))
        if after is None:
            weights[i] = ahead[i] * norm
            after = gaps[i]
        else:
            weights[i] = (after if i == 0 else ahead[i] * after) * norm
            after = after * gaps[i]
    return weights


def gather_matrix(rows):
    nodes = nodes_of(WIDE)
    index = np.arange(rows // BLOCK * WIDE)
    end = (index // WIDE + 1) * BLOCK - 1
    lag = end[:, None] - np.arange(rows)[None, :]
    return np.where(lag >= 0, np.exp(-nodes[index % WIDE][:, None] * np.maximum(lag, 0)), 0.0)


def spread_matrix(rows):
    nodes = nodes_of(WIDE)
    blocks = rows // BLOCK
    index = np.arange(blocks * WIDE)
    group = index // WIDE
    place = np.arange(rows)[:, None]
    end = np.where(group == blocks - 1, -1, (group + 1) * BLOCK - 1)[None, :]
    used = (group == blocks - 1)[None, :] | (place // BLOCK == group[None, :] + 1)
    lag = place - end
    return np.where(used, np.exp(-nodes[index % WIDE][None, :] * np.maximum(lag, 0)), 0.0)


def near_matrices(rows):
    lag = np.arange(rows)[:, None] - np.arange(rows)[None, :]
    same = (np.arange(rows)[:, None] // BLOCK == np.arange(rows)[None, :] // BLOCK) & (lag >= 0)
    return np.stack(
        [np.where(same, np.exp(-node * np.maximum(lag, 0)), 0.0) for node in nodes_of(NEAR)]
    )


def bounds_of(lengths_ref, anchor):
    total = -anchor
    bounds = []
    for i in range(lengths_ref.shape[0] - 1):
        total = total + lengths_ref[i]
        bounds.append(total)
    return bounds


def seg_of(place, bounds):
    return sum((place >= b).astype(jnp.int32) for b in bounds)


def halves(value):
    high = value.astype(BF16)
    return high, (value - high.astype(F32)).astype(BF16)


def product_of(left, right):
    return jnp.dot(left, right, preferred_element_type=F32)


def wide(column, columns):
    return jnp.concatenate([column] * (columns // column.shape[1]), axis=1)


def fill_keeps(keep_ref, bounds):
    rows = keep_ref.shape[1]
    place = lax.broadcasted_iota(jnp.int32, (rows, 128), 0)
    segment = seg_of(place, bounds)
    for i in range(2):
        keep_ref[i] = (seg_of(place - (i + 1), bounds) == segment).astype(F32)


def mix(block, edge, taps, keep_ref):
    rows, columns = block.shape
    now = block.astype(F32)
    edge = edge.astype(F32)
    row = lax.broadcasted_iota(jnp.int32, (rows, columns), 0)
    one = jnp.where(row == 0, edge[1:2], pltpu.roll(now, 1, 0))
    two = pltpu.roll(now, 2, 0)
    two = jnp.where(row == 0, edge[0:1], jnp.where(row == 1, edge[1:2], two))
    return (
        taps[0:1] * now
        + taps[1:2] * (one * wide(keep_ref[0], columns))
        + taps[2:3] * (two * wide(keep_ref[1], columns))
    )


def ends_kernel(
    lengths_ref, key_ref, value_ref, edge_ref, taps_ref, rate_ref, gather_ref, state_ref, keep_ref, matrix_ref
):
    rows = key_ref.shape[1]
    bounds = bounds_of(lengths_ref, lax.axis_index("ctx") * rows)

    @pl.when(pl.program_id(0) == 0)
    def _():
        fill_keeps(keep_ref, bounds)
        place = lax.broadcasted_iota(jnp.int32, (WIDE, rows), 1)
        same = seg_of(place, bounds) == seg_of(jnp.full((WIDE, rows), rows - 1, jnp.int32), bounds)
        high, low = halves(jnp.where(same, gather_ref[...], 0.0))
        matrix_ref[:WIDE] = high
        matrix_ref[WIDE:] = low

    product = mix(key_ref[0], edge_ref[1], taps_ref[:, 1], keep_ref) * mix(
        value_ref[0], edge_ref[2], taps_ref[:, 2], keep_ref
    )
    high, low = halves(product)
    moments = product_of(matrix_ref[...], high)
    moments = moments[:WIDE] + moments[WIDE:] + product_of(matrix_ref[:WIDE], low)
    weights = lagrange(rate_ref[...], nodes_of(WIDE))
    state = weights[0] * moments[0:1]
    for i in range(1, WIDE):
        state = state + weights[i] * moments[i : i + 1]
    state_ref[...] = state.astype(BF16)


def chain_kernel(rows, lengths_ref, local_ref, rate_ref, out_ref):
    fade = jnp.exp(-rate_ref[...] * F32(rows))
    bounds = bounds_of(lengths_ref, 0)
    state = jnp.zeros(rate_ref.shape, F32)
    for i in range(local_ref.shape[0]):
        out_ref[i] = state.astype(BF16)
        whole = seg_of(jnp.int32((i + 1) * rows - 1), bounds) == seg_of(jnp.int32(i * rows - 1), bounds)
        state = state * fade * whole.astype(F32) + local_ref[i].astype(F32)


def output_kernel(
    fused,
    lengths_ref,
    query_ref,
    key_ref,
    value_ref,
    edge_ref,
    taps_ref,
    rate_ref,
    residue_ref,
    skip_ref,
    gain_ref,
    arrived_ref,
    gather_ref,
    spread_ref,
    near_ref,
    out_ref,
    square_ref,
    keep_ref,
    gather_m,
    spread_m,
    near_m,
    held_ref,
):
    rows, columns = query_ref.shape[1:]
    phase, step = pl.program_id(0), pl.program_id(1)
    bounds = bounds_of(lengths_ref, lax.axis_index("ctx") * rows)

    @pl.when((phase == 0) & (step == 0))
    def _():
        fill_keeps(keep_ref, bounds)
        square_ref[...] = jnp.zeros_like(square_ref)
        across = lax.broadcasted_iota(jnp.int32, (rows, rows), 1)
        down = lax.broadcasted_iota(jnp.int32, (rows, rows), 0)
        count = gather_ref.shape[0]
        group = lax.broadcasted_iota(jnp.int32, (count, rows), 0) // WIDE
        same = seg_of(lax.broadcasted_iota(jnp.int32, (count, rows), 1), bounds) == seg_of(
            group * BLOCK + (BLOCK - 1), bounds
        )
        high, low = halves(jnp.where(same, gather_ref[...], 0.0))
        gather_m[:count] = high
        gather_m[count:] = low
        group = lax.broadcasted_iota(jnp.int32, (rows, count), 1) // WIDE
        end = jnp.where(group == rows // BLOCK - 1, -1, group * BLOCK + (BLOCK - 1))
        same = seg_of(lax.broadcasted_iota(jnp.int32, (rows, count), 0), bounds) == seg_of(end, bounds)
        high, low = halves(jnp.where(same, spread_ref[...], 0.0))
        spread_m[:, :count] = high
        spread_m[:, count:] = low
        same = seg_of(down, bounds) == seg_of(across, bounds)
        for i in range(NEAR):
            near_m[i] = jnp.where(same, near_ref[i].astype(F32), 0.0).astype(BF16)

    @pl.when(phase == 0)
    def _():
        query = mix(query_ref[0], edge_ref[0], taps_ref[:, 0], keep_ref)
        product = mix(key_ref[0], edge_ref[1], taps_ref[:, 1], keep_ref) * mix(
            value_ref[0], edge_ref[2], taps_ref[:, 2], keep_ref
        )
        rate = rate_ref[...]
        scale = residue_ref[...] * jnp.sqrt(1.0 - jnp.exp(-2.0 * rate))
        brought = scale * arrived_ref[...].astype(F32)
        weights = lagrange(rate, nodes_of(WIDE))
        share = jnp.concatenate([jnp.sum(w * scale, axis=0, keepdims=True) for w in weights], axis=0)
        entry = jnp.concatenate([jnp.sum(w * brought, axis=0, keepdims=True) for w in weights], axis=0)
        near = [jnp.sum(w * scale, axis=0, keepdims=True) for w in lagrange(rate, nodes_of(NEAR))]
        high, low = halves(product)
        total = skip_ref[...] * product
        for i in range(NEAR):
            total = total + near[i] * product_of(near_m[i], high)
        count = gather_ref.shape[0]
        moments = product_of(gather_m[...], high)
        moments = moments[:count] + moments[count:] + product_of(gather_m[:count], low)
        last = count - WIDE
        moments = (moments[:last].reshape(-1, WIDE, columns) * share[None]).reshape(last, columns)
        high, low = halves(jnp.concatenate([moments, entry], axis=0))
        total = total + product_of(spread_m[...], jnp.concatenate([high, high], axis=0))
        total = total + product_of(spread_m[:, :count], low)
        response = query * total
        squares = response * response
        part = squares[:, :128]
        for i in range(1, columns // 128):
            part = part + squares[:, i * 128 : (i + 1) * 128]
        square_ref[...] += part
        if fused:
            held_ref[step] = response
        else:
            out_ref[...] = response

    if fused:

        @pl.when((phase == 1) & (step == 0))
        def _():
            mean = jnp.sum(square_ref[...], axis=1, keepdims=True) / D
            square_ref[...] = jnp.broadcast_to(lax.rsqrt(mean + eps_norm), square_ref.shape)

        @pl.when(phase == 1)
        def _():
            out_ref[...] = (held_ref[step] * wide(square_ref[...], columns) * gain_ref[...]).astype(BF16)


def shards(features, short_taps, decay_rate, residue, skip_gain, norm_gain, contig_lengths):
    rows, _, channels = features.shape
    count = lax.axis_size("ctx")
    fused = lax.axis_size("chan") == 1
    poles = decay_rate.shape[0]
    planes = jnp.transpose(features, (1, 0, 2))
    columns = min(512, channels)
    steps = channels // columns
    edge = lax.ppermute(features[rows - 2 :], "ctx", [(i, i + 1) for i in range(count - 1)])
    edge = jnp.transpose(edge, (1, 0, 2))
    gather = jnp.asarray(gather_matrix(rows), F32)
    spread = jnp.asarray(spread_matrix(rows), F32)
    near = jnp.asarray(near_matrices(rows), BF16)
    smem = pl.BlockSpec(memory_space=pltpu.SMEM)

    def plane(i):
        return pl.BlockSpec((1, rows, columns), lambda j: (i, 0, j))

    ends = pl.pallas_call(
        ends_kernel,
        grid=(steps,),
        in_specs=[
            smem,
            plane(1),
            plane(2),
            pl.BlockSpec((3, 2, columns), lambda j: (0, 0, j)),
            pl.BlockSpec((3, 3, columns), lambda j: (0, 0, j)),
            pl.BlockSpec((poles, columns), lambda j: (0, j)),
            pl.BlockSpec((WIDE, rows), lambda j: (rows // BLOCK - 1, 0)),
        ],
        out_specs=pl.BlockSpec((poles, columns), lambda j: (0, j)),
        out_shape=jax.ShapeDtypeStruct((poles, channels), BF16),
        scratch_shapes=[pltpu.VMEM((2, rows, 128), F32), pltpu.VMEM((2 * WIDE, rows), BF16)],
        compiler_params=pltpu.CompilerParams(vmem_limit_bytes=40 << 20),
        name="ends",
    )(contig_lengths, planes, planes, edge, short_taps, decay_rate, gather)

    slim = channels // count
    pieces = lax.all_to_all(ends.reshape(poles, count, slim), "ctx", 1, 0, tiled=False)
    mine = lax.dynamic_slice_in_dim(decay_rate, lax.axis_index("ctx") * slim, slim, 1)
    chained = pl.pallas_call(
        functools.partial(chain_kernel, rows),
        in_specs=[smem, pl.BlockSpec(memory_space=pltpu.VMEM), pl.BlockSpec(memory_space=pltpu.VMEM)],
        out_specs=pl.BlockSpec(memory_space=pltpu.VMEM),
        out_shape=jax.ShapeDtypeStruct((count, poles, slim), BF16),
        name="chain",
    )(contig_lengths, pieces, mine)
    arrived = lax.all_to_all(chained, "ctx", 0, 1, tiled=False).reshape(poles, channels)

    def at(phase, j):
        return jnp.where(phase == 0, j, steps - 1)

    def per_block(shape):
        lead = (0,) * (len(shape) - 1)
        return pl.BlockSpec(shape, lambda phase, j: lead + (at(phase, j),))

    def plane_two(i):
        return pl.BlockSpec((1, rows, columns), lambda phase, j: (i, 0, at(phase, j)))

    def still(array):
        return pl.BlockSpec(array.shape, lambda phase, j: (0,) * array.ndim)

    if fused:
        out_map = lambda phase, j: (0, jnp.where(phase == 0, 0, j))
    else:
        out_map = lambda phase, j: (0, j)
    result, squares = pl.pallas_call(
        functools.partial(output_kernel, fused),
        grid=(2 if fused else 1, steps),
        in_specs=[
            smem,
            plane_two(0),
            plane_two(1),
            plane_two(2),
            per_block((3, 2, columns)),
            per_block((3, 3, columns)),
            per_block((poles, columns)),
            per_block((poles, columns)),
            per_block((1, columns)),
            pl.BlockSpec((1, columns), lambda phase, j: (0, j)),
            per_block((poles, columns)),
            still(gather),
            still(spread),
            still(near),
        ],
        out_specs=[pl.BlockSpec((rows, columns), out_map), pl.BlockSpec((rows, 128), lambda phase, j: (0, 0))],
        out_shape=[
            jax.ShapeDtypeStruct((rows, channels), BF16 if fused else F32),
            jax.ShapeDtypeStruct((rows, 128), F32),
        ],
        scratch_shapes=[
            pltpu.VMEM((2, rows, 128), F32),
            pltpu.VMEM((2 * gather.shape[0], rows), BF16),
            pltpu.VMEM((rows, 2 * spread.shape[1]), BF16),
            pltpu.VMEM(near.shape, BF16),
            pltpu.VMEM((steps, rows, columns) if fused else (1, 8, 128), F32),
        ],
        compiler_params=pltpu.CompilerParams(vmem_limit_bytes=48 << 20),
        name="output",
    )(
        contig_lengths,
        planes,
        planes,
        planes,
        edge,
        short_taps,
        decay_rate,
        residue,
        skip_gain.reshape(1, channels),
        norm_gain.reshape(1, channels),
        arrived,
        gather,
        spread,
        near,
    )
    if fused:
        return result
    mean = lax.psum(jnp.sum(squares, axis=1, keepdims=True), "chan") / D
    return (result * lax.rsqrt(mean + eps_norm) * norm_gain[None, :]).astype(BF16)


def solution(mesh):
    placed = (
        P("ctx", None, "chan"),
        P(None, None, "chan"),
        P(None, "chan"),
        P(None, "chan"),
        P("chan"),
        P("chan"),
        P(),
    )
    return jax.shard_map(
        shards, mesh=mesh, in_specs=placed, out_specs=P("ctx", "chan"), check_vma=False
    )
```

time: 792 us -> 105 us (0.13)
  matrix products: 373 us -> 0 us
  other arithmetic: 261 us -> 0 us
  waiting for transfers between devices: 117 us -> 10.9 us
  Pallas kernels: 0 us -> 56.5 us
  between operations: 13.6 us -> 0.17 us
  blocking collectives: 0 us -> 13.2 us
  starting transfers between devices: 2.41 us -> 12.3 us
  local copies, waits for them, and re-layouts: 20.3 us -> 11.5 us
    dot_general x32 -> x0, matrix products: 373 us -> none  [one_mode(): jnp.dot(lower_mask, scaled, precision=lax.Precision.HIGHEST, preferred_el...]
    all_gather x2 -> x0, waiting for transfers between devices: 117 us -> none  [carried_in(): pieces = jax.tree.map(lambda part: lax.all_gather(part, axis), value)]
    reduce_sum x4 -> x0, other arithmetic: 60.5 us -> none  [the longest x1 41.7 us: shards(): jnp.sum(jnp.exp(-decay_rate[None, :, :] * offsets[:, None, None]) * weigh...]
    pallas_call x0 -> x3, Pallas kernels: none -> 56.5 us  [the longest x1 41.2 us: shards(): pl.pallas_call(functools.partial(output_kernel, fused), grid=(2 if fused...]
    select_n x31 -> x0, other arithmetic: 51.3 us -> none  [turn(): jnp.where(position < mine, new, old)]
    another operation x65 -> x0, other arithmetic: 45.2 us -> none
    neg x33 -> x0, other arithmetic: 35.4 us -> none  [the longest x32 32.6 us: one_mode(): -rate_row[None, :] * steps_in[:, None]]
    add x35 -> x0, other arithmetic: 35.3 us -> none  [the longest x1 35 us: shards(): short_taps[0] * extended[2:]]
  transfers between devices with their start and end apart: 3 -> 2, of which waited for: 1 -> 2; matrix products, arithmetic and copies ran while one was open for 68% -> 1% of each run, Pallas kernels for 0% -> 0%
where the time goes in v1:
time: 105 us
  Pallas kernels  56.5 us (54%)
  blocking collectives  13.2 us (13%)
  starting transfers between devices  12.3 us (12%)
  local copies, waits for them, and re-layouts  11.5 us (11%)
  waiting for transfers between devices  10.9 us (10%)
    pallas_call x1, Pallas kernels, shards(): pl.pallas_call(functools.partial(output_kernel, fused), grid=(2 if fused...  41.2 us
    pallas_call x1, Pallas kernels, shards(): pl.pallas_call(ends_kernel, grid=(steps,), in_specs=[smem, plane(1), plan...  13.4 us
    all_to_all x1, blocking collectives, shards(): lax.all_to_all(chained, 'ctx', 0, 1, tiled=False).reshape(poles, channels)  13.2 us
    all_to_all x1, waiting for transfers between devices, shards(): lax.all_to_all(ends.reshape(poles, count, slim), 'ctx', 1, 0, tiled=False)  9.97 us
    all_to_all x1, starting transfers between devices, shards(): lax.all_to_all(ends.reshape(poles, count, slim), 'ctx', 1, 0, tiled=False)  9.94 us
    unnamed x32, local copies, waits for them, and re-layouts  8.98 us
    ppermute x1, starting transfers between devices, shards(): lax.ppermute(features[rows - 2:], 'ctx', [(i, i + 1) for i in range(count...  2.36 us
  transfers between devices with their start and end apart: 2, of which 2 were waited for; matrix products, arithmetic and copies ran while one was open for 1% of the time, Pallas kernels for 0%

profile of v1, /device:TPU:0, one launch (start us, length us, event | category | flops | bytes accessed | tf_op | source)
XLA Modules:
  0.0 104.6 jit_solution(8223299468751139321)
XLA Ops:
  0.0 1.1 %slice.3 = bf16[2,3,8192]{2,0,1:T(2,128)(2,1)S(1)} slice(bf16[256,3,8192]{2,0,1:T(8,128)(2,1)} %param.10), slice={[254:256], [0:3], [0:8192]} | slice | bytes 196608 | tf_op jit(solution)/shard_map/slice | solution.py:270
  1.1 2.4 %collective-permute-start = (bf16[2,3,8192]{2,0,1:T(2,128)(2,1)S(1)}, bf16[2,3,8192]{2,0,1:T(2,128)(2,1)S(1)}, u32[]{:S(2)}, u32[]{:S(2)}) collective-permute-start(bf16[2,3,8192]{2,0,1:T(2,128)(2,1)S(1)} %slice.3), channel_id=1, source_target_pairs={{0,1},{1,2},{2,3},{3,4},{4,5},{5,6},{6,7},{7,8},{8,9},{9,10},{10,1... | collective-permute-start | bytes 294920 | tf_op jit(solution)/shard_map/ppermute | solution.py:270
  3.5 0.9 collective-permute-done
  4.4 0.0 copy-start
  4.4 4.6 %copy-done = bf16[256,3,8192]{2,0,1:T(8,128)(2,1)S(1)} copy-done((bf16[256,3,8192]{2,0,1:T(8,128)(2,1)S(1)}, bf16[256,3,8192]{2,0,1:T(8,128)(2,1)}, u32[]{:S(2)}) %copy-start) | copy-done | bytes 12582936
  9.0 0.0 copy-start.1
  9.0 1.0 copy-done.1
  10.0 0.0 copy-start.3
  10.0 1.0 copy-done.3
  11.0 0.0 copy-start.7
  11.0 0.9 copy-done.7
  11.9 0.0 copy-start.12
  11.9 0.7 copy-done.12
  12.6 0.0 copy-start.2
  12.6 0.0 copy-start.4
  12.6 0.0 copy-start.5
  12.6 0.0 copy-start.6
  12.6 0.0 copy-start.8
  12.6 0.0 copy-start.9
  12.6 0.0 copy-start.10
  12.6 0.0 copy-start.11
  12.6 0.0 copy-start.13
  12.6 13.4 %ends.1 = bf16[16,8192]{1,0:T(8,128)(2,1)S(1)} custom-call(s32[4]{0:T(128)S(1)} %copy-done.12, bf16[3,256,8192]{2,1,0:T(8,128)(2,1)S(1)} %bitcast.27, bf16[3,256,8192]{2,1,0:T(8,128)(2,1)S(1)} %bitcast.28, bf16[3,2,8192]{2,1,0:T(2,128)(2,1)S(1)} %bitcast.31, f32[3,3,8192]{2,1,0:T(4,128)S(1)} %copy-done.3, f32[16,8192]{1,0:T(8,128)S(1)} %copy-done.1, ...), custom_call_target="tpu_custom_call" | custom-call | tf_op jit(solution)/shard_map/ends/pallas_call | solution.py:280
  26.2 0.9 copy.14
  27.0 9.9 %all-to-all-start = ((bf16[1,16,32,256]{3,1,0,2:T(8,128)(2,1)}), bf16[1,16,32,256]{3,1,0,2:T(8,128)(2,1)S(1)}, u32[]{:S(2)}, u32[]{:S(2)}) async-start(bf16[1,16,32,256]{3,1,0,2:T(8,128)(2,1)} %copy.14), calls=%async_computation | async-start | bytes 524288 | tf_op jit(solution)/shard_map/all_to_all | solution.py:300
  37.0 0.0 copy-done.2
  37.0 0.6 constant_dynamic-slice_fusion.rate_ref
  37.6 10.0 %all-to-all-done = bf16[1,16,32,256]{3,1,0,2:T(8,128)(2,1)S(1)} async-done(((bf16[1,16,32,256]{3,1,0,2:T(8,128)(2,1)}), bf16[1,16,32,256]{3,1,0,2:T(8,128)(2,1)S(1)}, u32[]{:S(2)}, u32[]{:S(2)}) %all-to-all-start) | async-done | bytes 262176 | tf_op jit(solution)/shard_map/all_to_all | solution.py:300
  47.6 0.0 copy-start.14
  47.6 0.7 copy-done.14
  48.3 1.8 %chain.1 = bf16[32,16,256]{2,1,0:T(8,128)(2,1)} custom-call(s32[4]{0:T(128)} %lengths_ref.5, bf16[32,16,256]{2,1,0:T(8,128)(2,1)} %bitcast.35, f32[16,256]{1,0:T(8,128)} %constant_dynamic-slice_fusion.rate_ref), custom_call_target="tpu_custom_call" | custom-call | tf_op jit(solution)/shard_map/chain/pallas_call | solution.py:302
  50.1 13.2 %all_to_all.30 = bf16[32,16,1,256]{3,1,2,0:T(8,128)(2,1)S(1)} all-to-all(bf16[32,16,1,256]{3,1,2,0:T(8,128)(2,1)} %bitcast.36), channel_id=1, replica_groups=mesh['ctx'=32,'chan'=1] {'ctx'}, dimensions={0} | all-to-all | bytes 524288 | tf_op jit(solution)/shard_map/all_to_all | solution.py:309
  63.3 0.0 copy-done.4
  63.3 0.0 copy-done.5
  63.3 0.0 copy-done.6
  63.3 0.0 copy-done.8
  63.3 0.0 copy-done.9
  63.3 0.0 copy-done.10
  63.3 0.0 copy-done.11
  63.3 0.0 copy-done.13
  63.3 41.2 %output.1 = (bf16[256,8192]{1,0:T(8,128)(2,1)}, f32[256,128]{1,0:T(8,128)}) custom-call(s32[4]{0:T(128)S(1)} %copy-done.13, bf16[3,256,8192]{2,1,0:T(8,128)(2,1)} %bitcast.24, bf16[3,256,8192]{2,1,0:T(8,128)(2,1)} %bitcast.25, bf16[3,256,8192]{2,1,0:T(8,128)(2,1)} %bitcast.26, bf16[3,2,8192]{2,1,0:T(2,128)(2,1)S(1)} %bitcast.32, ...), custom_call_target="tpu_custom_call" | custom-call | tf_op jit(solution)/shard_map/output/pallas_call | solution.py:328
  (2 shorter events, 0.1 us)
Async XLA Ops:
  1.1 3.3 %collective-permute-start = (bf16[2,3,8192]{2,0,1:T(2,128)(2,1)S(1)}, bf16[2,3,8192]{2,0,1:T(2,128)(2,1)S(1)}, u32[]{:S(2)}, u32[]{:S(2)}) collective-permute-start(bf16[2,3,8192]{2,0,1:T(2,128)(2,1)S(1)} %slice.3), channel_id=1, source_target_pairs={{0,1},{1,2},{2,3},{3,4},{4,5},{5,6},{6,7},{7,8},{8,9},{9,10},{10,1... | collective-permute-start | bytes 294920 | tf_op jit(solution)/shard_map/ppermute | solution.py:270
  4.4 4.6 %copy-start = (bf16[256,3,8192]{2,0,1:T(8,128)(2,1)S(1)}, bf16[256,3,8192]{2,0,1:T(8,128)(2,1)}, u32[]{:S(2)}) copy-start(bf16[256,3,8192]{2,0,1:T(8,128)(2,1)} %param.10) | copy-start | bytes 37748740
  9.0 1.0 copy-start.1
  10.0 1.0 copy-start.3
  11.0 0.9 copy-start.7
  11.9 0.7 copy-start.12
  12.6 24.4 %copy-start.2 = (f32[16,8192]{1,0:T(8,128)S(1)}, f32[16,8192]{1,0:T(8,128)}, u32[]{:S(2)}) copy-start(f32[16,8192]{1,0:T(8,128)} %rate_ref.3) | copy-start | bytes 1572868
  12.6 50.7 %copy-start.4 = (f32[3,3,8192]{2,1,0:T(4,128)S(1)}, f32[3,3,8192]{2,1,0:T(4,128)}, u32[]{:S(2)}) copy-start(f32[3,3,8192]{2,1,0:T(4,128)} %taps_ref.3) | copy-start | bytes 884740
  12.6 50.7 %copy-start.5 = (bf16[7,256,256]{2,1,0:T(8,128)(2,1)S(1)}, bf16[7,256,256]{2,1,0:T(8,128)(2,1)}, u32[]{:S(2)}) copy-start(bf16[7,256,256]{2,1,0:T(8,128)(2,1)} %constant.18.clone.near_ref) | copy-start | bytes 2752516
  12.6 50.7 %copy-start.6 = (f32[16,8192]{1,0:T(8,128)S(1)}, f32[16,8192]{1,0:T(8,128)}, u32[]{:S(2)}) copy-start(f32[16,8192]{1,0:T(8,128)} %residue_ref.1) | copy-start | bytes 1572868
  12.6 50.7 %copy-start.8 = (f32[128,256]{1,0:T(8,128)S(1)}, f32[128,256]{1,0:T(8,128)}, u32[]{:S(2)}) copy-start(f32[128,256]{1,0:T(8,128)} %constant.16.clone.gather_ref) | copy-start | bytes 393220
  12.6 50.7 %copy-start.9 = (f32[256,128]{1,0:T(8,128)S(1)}, f32[256,128]{1,0:T(8,128)}, u32[]{:S(2)}) copy-start(f32[256,128]{1,0:T(8,128)} %constant.17.clone.spread_ref) | copy-start | bytes 393220
  12.6 50.7 %copy-start.10 = (f32[8192]{0:T(1024)S(1)}, f32[8192]{0:T(1024)}, u32[]{:S(2)}) copy-start(f32[8192]{0:T(1024)} %param.14) | copy-start | bytes 98308
  12.6 50.7 %copy-start.11 = (f32[8192]{0:T(1024)S(1)}, f32[8192]{0:T(1024)}, u32[]{:S(2)}) copy-start(f32[8192]{0:T(1024)} %param.15) | copy-start | bytes 98308
  12.6 50.7 %copy-start.13 = (s32[4]{0:T(128)S(1)}, s32[4]{0:T(128)}, u32[]{:S(2)}) copy-start(s32[4]{0:T(128)} %lengths_ref.5) | copy-start | bytes 52
  27.0 20.5 %all-to-all-start = ((bf16[1,16,32,256]{3,1,0,2:T(8,128)(2,1)}), bf16[1,16,32,256]{3,1,0,2:T(8,128)(2,1)S(1)}, u32[]{:S(2)}, u32[]{:S(2)}) async-start(bf16[1,16,32,256]{3,1,0,2:T(8,128)(2,1)} %copy.14), calls=%async_computation | async-start | bytes 524288 | tf_op jit(solution)/shard_map/all_to_all | solution.py:300
  47.6 0.7 copy-start.14

commit v2 on v1

--- a/solution.py
+++ b/solution.py
@@ -14,6 +14,8 @@
 BLOCK = 32
 WIDE = 16
 NEAR = 7
+TEAM = 8
+CHUNK = 256
 F32 = jnp.float32
 BF16 = jnp.bfloat16
 
@@ -121,42 +123,173 @@
     )
 
 
-def ends_kernel(
-    lengths_ref, key_ref, value_ref, edge_ref, taps_ref, rate_ref, gather_ref, state_ref, keep_ref, matrix_ref
+def exchange_kernel(
+    lengths_ref,
+    planes_ref,
+    taps_ref,
+    rate_ref,
+    gather_ref,
+    arrived_ref,
+    edge_ref,
+    keep_ref,
+    matrix_ref,
+    rows_ref,
+    tail_ref,
+    edge_send,
+    edge_land,
+    local_send,
+    local_land,
+    total_land,
+    back_send,
+    back_land,
+    rows_sem,
+    tail_sem,
+    edge_sem,
+    local_sem,
+    total_sem,
+    back_sem,
 ):
-    rows = key_ref.shape[1]
-    bounds = bounds_of(lengths_ref, lax.axis_index("ctx") * rows)
-
-    @pl.when(pl.program_id(0) == 0)
-    def _():
-        fill_keeps(keep_ref, bounds)
-        place = lax.broadcasted_iota(jnp.int32, (WIDE, rows), 1)
-        same = seg_of(place, bounds) == seg_of(jnp.full((WIDE, rows), rows - 1, jnp.int32), bounds)
-        high, low = halves(jnp.where(same, gather_ref[...], 0.0))
-        matrix_ref[:WIDE] = high
-        matrix_ref[WIDE:] = low
-
-    product = mix(key_ref[0], edge_ref[1], taps_ref[:, 1], keep_ref) * mix(
-        value_ref[0], edge_ref[2], taps_ref[:, 2], keep_ref
-    )
-    high, low = halves(product)
-    moments = product_of(matrix_ref[...], high)
-    moments = moments[:WIDE] + moments[WIDE:] + product_of(matrix_ref[:WIDE], low)
-    weights = lagrange(rate_ref[...], nodes_of(WIDE))
-    state = weights[0] * moments[0:1]
-    for i in range(1, WIDE):
-        state = state + weights[i] * moments[i : i + 1]
-    state_ref[...] = state.astype(BF16)
-
-
-def chain_kernel(rows, lengths_ref, local_ref, rate_ref, out_ref):
-    fade = jnp.exp(-rate_ref[...] * F32(rows))
-    bounds = bounds_of(lengths_ref, 0)
-    state = jnp.zeros(rate_ref.shape, F32)
-    for i in range(local_ref.shape[0]):
-        out_ref[i] = state.astype(BF16)
-        whole = seg_of(jnp.int32((i + 1) * rows - 1), bounds) == seg_of(jnp.int32(i * rows - 1), bounds)
-        state = state * fade * whole.astype(F32) + local_ref[i].astype(F32)
+    rows, channels = planes_ref.shape[1:]
+    half = channels // 2
+    count = lax.axis_size("ctx")
+    teams = count // TEAM
+    slim = channels // TEAM
+    chunk = min(CHUNK, slim)
+    me = lax.axis_index("ctx")
+    team, rank = me // TEAM, me % TEAM
+
+    def mate(k):
+        return team * TEAM + (rank + k) % TEAM
+
+    def peer(k):
+        return (team + k) % teams * TEAM + rank
+
+    def span(k):
+        return pl.ds(pl.multiple_of((rank + k) % TEAM * slim, 128), slim)
+
+    def load(k):
+        return pltpu.make_async_copy(
+            planes_ref.at[pl.ds(1, 2), :, span(k)], rows_ref.at[:, :, span(k)], rows_sem.at[k]
+        )
+
+    tail = pltpu.make_async_copy(planes_ref.at[:, pl.ds(rows - 16, 16), :], tail_ref, tail_sem)
+    tail.start()
+    for k in range(TEAM):
+        load((k + 1) % TEAM).start()
+
+    barrier = pltpu.get_barrier_semaphore()
+    others = [mate(k) for k in range(1, TEAM)] + [peer(k) for k in range(1, teams)]
+    others += [(me + 1) % count, (me + count - 1) % count]
+    for other in others:
+        pl.semaphore_signal(barrier, inc=1, device_id={"ctx": other}, device_id_type=pl.DeviceIdType.MESH)
+
+    bounds = bounds_of(lengths_ref, me * rows)
+    zero_bounds = bounds_of(lengths_ref, 0)
+    fill_keeps(keep_ref, bounds)
+    place = lax.broadcasted_iota(jnp.int32, (WIDE, rows), 1)
+    same = seg_of(place, bounds) == seg_of(jnp.full((WIDE, rows), rows - 1, jnp.int32), bounds)
+    high, low = halves(jnp.where(same, gather_ref[...], 0.0))
+    matrix_ref[:WIDE] = high
+    matrix_ref[WIDE:] = low
+    tail.wait()
+    ends = [tail_ref[i].astype(F32)[14:16] for i in range(3)]
+    packed = [e[:, :half] for e in ends] + [e[:, half:] for e in ends] + [jnp.zeros((4, half), F32)]
+    edge_send[...] = jnp.concatenate(packed, axis=0).astype(BF16)
+
+    def remote(source, target, sems, device):
+        return pltpu.make_async_remote_copy(
+            src_ref=source,
+            dst_ref=target,
+            send_sem=sems[0],
+            recv_sem=sems[1],
+            device_id={"ctx": device},
+            device_id_type=pl.DeviceIdType.MESH,
+        )
+
+    pl.semaphore_wait(barrier, len(others))
+    edge_copy = remote(edge_send, edge_land, (edge_sem.at[0], edge_sem.at[1]), (me + 1) % count)
+    edge_copy.start()
+    edge_copy.wait()
+    landed = jnp.where(me == 0, 0.0, edge_land[...].astype(F32))
+    blank = jnp.zeros((2, half), F32)
+    edge_ref[:, :half] = jnp.concatenate([landed[0:6], blank], axis=0)
+    edge_ref[:, half:] = jnp.concatenate([landed[6:12], blank], axis=0)
+
+    def local_copy(k):
+        return remote(local_send.at[k], local_land.at[k], (local_sem.at[k, 0], local_sem.at[k, 1]), mate(k))
+
+    def one_slice(k, into):
+        load(k).wait()
+        base = (rank + k) % TEAM * slim
+
+        def one_chunk(i, carry):
+            here = pl.ds(pl.multiple_of(base + i * chunk, 128), chunk)
+            key = mix(rows_ref[0, :, here], edge_ref[2:4, here], taps_ref[:, 1, here], keep_ref)
+            value = mix(rows_ref[1, :, here], edge_ref[4:6, here], taps_ref[:, 2, here], keep_ref)
+            high, low = halves(key * value)
+            moments = product_of(matrix_ref[...], high)
+            moments = moments[:WIDE] + moments[WIDE:] + product_of(matrix_ref[:WIDE], low)
+            weights = lagrange(rate_ref[:, here], nodes_of(WIDE))
+            state = weights[0] * moments[0:1]
+            for n in range(1, WIDE):
+                state = state + weights[n] * moments[n : n + 1]
+            into[k, :, pl.ds(pl.multiple_of(i * chunk, 128), chunk)] = state.astype(BF16)
+            return carry
+
+        lax.fori_loop(0, slim // chunk, one_chunk, 0)
+
+    def send_slice(k, carry):
+        one_slice(k, local_send)
+        local_copy(k).start()
+        return carry
+
+    lax.fori_loop(1, TEAM, send_slice, 0)
+    one_slice(0, local_land)
+
+    mine = pl.ds(pl.multiple_of(rank * slim, 128), slim)
+    rate = rate_ref[:, mine]
+    fade = jnp.exp(-rate * F32(rows))
+    fade_team = jnp.exp(-rate * F32(rows * TEAM))
+
+    def whole(first, devices):
+        start = first * rows
+        kept = seg_of(start + devices * rows - 1, zero_bounds) == seg_of(start - 1, zero_bounds)
+        return kept.astype(F32)
+
+    for k in range(1, TEAM):
+        local_copy(k).wait()
+    local = [local_land[(rank + TEAM - s) % TEAM].astype(F32) for s in range(TEAM)]
+    total = local[0]
+    for s in range(1, TEAM):
+        total = total * (fade * whole(team * TEAM + s, 1)) + local[s]
+    total_land[0] = total.astype(BF16)
+
+    def total_copy(k):
+        return remote(total_land.at[0], total_land.at[k], (total_sem.at[k, 0], total_sem.at[k, 1]), peer(k))
+
+    for k in range(1, teams):
+        total_copy(k).start()
+    for k in range(1, teams):
+        total_copy(k).wait()
+    state = jnp.zeros(rate.shape, F32)
+    for g in range(teams - 1):
+        after = state * (fade_team * whole(g * TEAM, TEAM)) + total_land[(team + teams - g) % teams].astype(F32)
+        state = jnp.where(g < team, after, state)
+    for s in range(TEAM):
+        back_send[s] = state.astype(BF16)
+        if s < TEAM - 1:
+            state = state * (fade * whole(team * TEAM + s, 1)) + local[s]
+
+    def back_copy(k):
+        return remote(back_send.at[(rank + k) % TEAM], back_land.at[k], (back_sem.at[k, 0], back_sem.at[k, 1]), mate(k))
+
+    for k in range(1, TEAM):
+        back_copy(k).start()
+    arrived_ref[:, mine] = back_send[rank]
+    for k in range(1, TEAM):
+        back_copy(k).wait()
+    for k in range(1, TEAM):
+        arrived_ref[:, span(TEAM - k)] = back_land[k]
 
 
 def output_kernel(
@@ -213,39 +346,45 @@
 
     @pl.when(phase == 0)
     def _():
-        query = mix(query_ref[0], edge_ref[0], taps_ref[:, 0], keep_ref)
-        product = mix(key_ref[0], edge_ref[1], taps_ref[:, 1], keep_ref) * mix(
-            value_ref[0], edge_ref[2], taps_ref[:, 2], keep_ref
-        )
-        rate = rate_ref[...]
-        scale = residue_ref[...] * jnp.sqrt(1.0 - jnp.exp(-2.0 * rate))
-        brought = scale * arrived_ref[...].astype(F32)
-        weights = lagrange(rate, nodes_of(WIDE))
-        share = jnp.concatenate([jnp.sum(w * scale, axis=0, keepdims=True) for w in weights], axis=0)
-        entry = jnp.concatenate([jnp.sum(w * brought, axis=0, keepdims=True) for w in weights], axis=0)
-        near = [jnp.sum(w * scale, axis=0, keepdims=True) for w in lagrange(rate, nodes_of(NEAR))]
-        high, low = halves(product)
-        total = skip_ref[...] * product
-        for i in range(NEAR):
-            total = total + near[i] * product_of(near_m[i], high)
-        count = gather_ref.shape[0]
-        moments = product_of(gather_m[...], high)
-        moments = moments[:count] + moments[count:] + product_of(gather_m[:count], low)
-        last = count - WIDE
-        moments = (moments[:last].reshape(-1, WIDE, columns) * share[None]).reshape(last, columns)
-        high, low = halves(jnp.concatenate([moments, entry], axis=0))
-        total = total + product_of(spread_m[...], jnp.concatenate([high, high], axis=0))
-        total = total + product_of(spread_m[:, :count], low)
-        response = query * total
-        squares = response * response
-        part = squares[:, :128]
-        for i in range(1, columns // 128):
-            part = part + squares[:, i * 128 : (i + 1) * 128]
-        square_ref[...] += part
-        if fused:
-            held_ref[step] = response
-        else:
-            out_ref[...] = response
+        chunk = min(CHUNK, columns)
+
+        def one_chunk(index, carry):
+            here = pl.ds(pl.multiple_of(index * chunk, 128), chunk)
+            product = mix(key_ref[0, :, here], edge_ref[2:4, here], taps_ref[:, 1, here], keep_ref) * mix(
+                value_ref[0, :, here], edge_ref[4:6, here], taps_ref[:, 2, here], keep_ref
+            )
+            rate = rate_ref[:, here]
+            scale = residue_ref[:, here] * jnp.sqrt(1.0 - jnp.exp(-2.0 * rate))
+            brought = scale * arrived_ref[:, here].astype(F32)
+            weights = lagrange(rate, nodes_of(WIDE))
+            share = jnp.concatenate([jnp.sum(w * scale, axis=0, keepdims=True) for w in weights], axis=0)
+            entry = jnp.concatenate([jnp.sum(w * brought, axis=0, keepdims=True) for w in weights], axis=0)
+            near = [jnp.sum(w * scale, axis=0, keepdims=True) for w in lagrange(rate, nodes_of(NEAR))]
+            high, low = halves(product)
+            total = skip_ref[:, here] * product
+            for i in range(NEAR):
+                total = total + near[i] * product_of(near_m[i], high)
+            count = gather_ref.shape[0]
+            moments = product_of(gather_m[...], high)
+            moments = moments[:count] + moments[count:] + product_of(gather_m[:count], low)
+            last = count - WIDE
+            moments = (moments[:last].reshape(-1, WIDE, chunk) * share[None]).reshape(last, chunk)
+            high, low = halves(jnp.concatenate([moments, entry], axis=0))
+            total = total + product_of(spread_m[...], jnp.concatenate([high, high], axis=0))
+            total = total + product_of(spread_m[:, :count], low)
+            response = mix(query_ref[0, :, here], edge_ref[0:2, here], taps_ref[:, 0, here], keep_ref) * total
+            squares = response * response
+            part = squares[:, :128]
+            for i in range(1, chunk // 128):
+                part = part + squares[:, i * 128 : (i + 1) * 128]
+            square_ref[...] += part
+            if fused:
+                held_ref[step, :, here] = response
+            else:
+                out_ref[:, here] = response
+            return carry
+
+        lax.fori_loop(0, columns // chunk, one_chunk, 0)
 
     if fused:
 
@@ -265,48 +404,48 @@
     fused = lax.axis_size("chan") == 1
     poles = decay_rate.shape[0]
     planes = jnp.transpose(features, (1, 0, 2))
-    columns = min(512, channels)
+    columns = min(1024, channels)
     steps = channels // columns
-    edge = lax.ppermute(features[rows - 2 :], "ctx", [(i, i + 1) for i in range(count - 1)])
-    edge = jnp.transpose(edge, (1, 0, 2))
     gather = jnp.asarray(gather_matrix(rows), F32)
     spread = jnp.asarray(spread_matrix(rows), F32)
     near = jnp.asarray(near_matrices(rows), BF16)
     smem = pl.BlockSpec(memory_space=pltpu.SMEM)
 
-    def plane(i):
-        return pl.BlockSpec((1, rows, columns), lambda j: (i, 0, j))
-
-    ends = pl.pallas_call(
-        ends_kernel,
-        grid=(steps,),
-        in_specs=[
-            smem,
-            plane(1),
-            plane(2),
-            pl.BlockSpec((3, 2, columns), lambda j: (0, 0, j)),
-            pl.BlockSpec((3, 3, columns), lambda j: (0, 0, j)),
-            pl.BlockSpec((poles, columns), lambda j: (0, j)),
-            pl.BlockSpec((WIDE, rows), lambda j: (rows // BLOCK - 1, 0)),
+    vmem = pl.BlockSpec(memory_space=pltpu.VMEM)
+    slim = channels // TEAM
+    teams = count // TEAM
+    arrived, edge = pl.pallas_call(
+        exchange_kernel,
+        in_specs=[smem, pl.BlockSpec(memory_space=pl.ANY), vmem, vmem, vmem],
+        out_specs=[vmem, vmem],
+        out_shape=[
+            jax.ShapeDtypeStruct((poles, channels), BF16),
+            jax.ShapeDtypeStruct((8, channels), F32),
         ],
-        out_specs=pl.BlockSpec((poles, columns), lambda j: (0, j)),
-        out_shape=jax.ShapeDtypeStruct((poles, channels), BF16),
-        scratch_shapes=[pltpu.VMEM((2, rows, 128), F32), pltpu.VMEM((2 * WIDE, rows), BF16)],
-        compiler_params=pltpu.CompilerParams(vmem_limit_bytes=40 << 20),
-        name="ends",
-    )(contig_lengths, planes, planes, edge, short_taps, decay_rate, gather)
-
-    slim = channels // count
-    pieces = lax.all_to_all(ends.reshape(poles, count, slim), "ctx", 1, 0, tiled=False)
-    mine = lax.dynamic_slice_in_dim(decay_rate, lax.axis_index("ctx") * slim, slim, 1)
-    chained = pl.pallas_call(
-        functools.partial(chain_kernel, rows),
-        in_specs=[smem, pl.BlockSpec(memory_space=pltpu.VMEM), pl.BlockSpec(memory_space=pltpu.VMEM)],
-        out_specs=pl.BlockSpec(memory_space=pltpu.VMEM),
-        out_shape=jax.ShapeDtypeStruct((count, poles, slim), BF16),
-        name="chain",
-    )(contig_lengths, pieces, mine)
-    arrived = lax.all_to_all(chained, "ctx", 0, 1, tiled=False).reshape(poles, channels)
+        scratch_shapes=[
+            pltpu.VMEM((2, rows, 128), F32),
+            pltpu.VMEM((2 * WIDE, rows), BF16),
+            pltpu.VMEM((2, rows, channels), BF16),
+            pltpu.VMEM((3, 16, channels), BF16),
+            pltpu.VMEM((16, channels // 2), BF16),
+            pltpu.VMEM((16, channels // 2), BF16),
+            pltpu.VMEM((TEAM, poles, slim), BF16),
+            pltpu.VMEM((TEAM, poles, slim), BF16),
+            pltpu.VMEM((teams, poles, slim), BF16),
+            pltpu.VMEM((TEAM, poles, slim), BF16),
+            pltpu.VMEM((TEAM, poles, slim), BF16),
+            pltpu.SemaphoreType.DMA((TEAM,)),
+            pltpu.SemaphoreType.DMA,
+            pltpu.SemaphoreType.DMA((2,)),
+            pltpu.SemaphoreType.DMA((TEAM, 2)),
+            pltpu.SemaphoreType.DMA((teams, 2)),
+            pltpu.SemaphoreType.DMA((TEAM, 2)),
+        ],
+        compiler_params=pltpu.CompilerParams(
+            collective_id=0, has_side_effects=True, vmem_limit_bytes=60 << 20
+        ),
+        name="exchange",
+    )(contig_lengths, planes, short_taps, decay_rate, jnp.asarray(gather_matrix(rows)[-WIDE:], F32))
 
     def at(phase, j):
         return jnp.where(phase == 0, j, steps - 1)
@@ -333,7 +472,7 @@
             plane_two(0),
             plane_two(1),
             plane_two(2),
-            per_block((3, 2, columns)),
+            per_block((8, columns)),
             per_block((3, 3, columns)),
             per_block((poles, columns)),
             per_block((poles, columns)),
@@ -356,7 +495,7 @@
             pltpu.VMEM(near.shape, BF16),
             pltpu.VMEM((steps, rows, columns) if fused else (1, 8, 128), F32),
         ],
-        compiler_params=pltpu.CompilerParams(vmem_limit_bytes=48 << 20),
+        compiler_params=pltpu.CompilerParams(vmem_limit_bytes=60 << 20),
         name="output",
     )(
         contig_lengths,

time: 105 us -> 75.8 us (0.72)
  Pallas kernels: 56.5 us -> 75.4 us
  blocking collectives: 13.2 us -> 0 us
  starting transfers between devices: 12.3 us -> 0 us
  local copies, waits for them, and re-layouts: 11.5 us -> 0 us
  waiting for transfers between devices: 10.9 us -> 0 us
    pallas_call x2 -> x1, Pallas kernels: 15.3 us -> 35.1 us  [shards(): pl.pallas_call(exchange_kernel, in_specs=[smem, pl.BlockSpec(memory_space...]
    all_to_all x1 -> x0, blocking collectives: 13.2 us -> none  [shards(): lax.all_to_all(chained, 'ctx', 0, 1, tiled=False).reshape(poles, channels)]
    all_to_all x1 -> x0, waiting for transfers between devices: 9.97 us -> none  [shards(): lax.all_to_all(ends.reshape(poles, count, slim), 'ctx', 1, 0, tiled=False)]
    all_to_all x1 -> x0, starting transfers between devices: 9.94 us -> none  [shards(): lax.all_to_all(ends.reshape(poles, count, slim), 'ctx', 1, 0, tiled=False)]
    unnamed x32 -> x0, local copies, waits for them, and re-layouts: 8.98 us -> none
    ppermute x1 -> x0, starting transfers between devices: 2.36 us -> none  [shards(): lax.ppermute(features[rows - 2:], 'ctx', [(i, i + 1) for i in range(count...]
    slice x1 -> x0, local copies, waits for them, and re-layouts: 1.1 us -> none  [shards(): features[rows - 2:]]
  transfers between devices with their start and end apart: 2 -> 0, of which waited for: 2 -> 0; matrix products, arithmetic and copies ran while one was open for 1% -> 0% of each run, Pallas kernels for 0% -> 0%
where the time goes in v2:
time: 75.8 us; the launch traced here: 75.4 us
  Pallas kernels  75.4 us (99%)
    pallas_call x1, Pallas kernels, shards(): pl.pallas_call(functools.partial(output_kernel, fused), grid=(2 if fused...  40.3 us
    pallas_call x1, Pallas kernels, shards(): pl.pallas_call(exchange_kernel, in_specs=[smem, pl.BlockSpec(memory_space...  35.1 us

profile of v2, /device:TPU:0, one launch (start us, length us, event | category | flops | bytes accessed | tf_op | source)
XLA Modules:
  0.0 75.4 jit_solution(10195067104633724910)
XLA Ops:
  0.0 35.1 %exchange.1 = (bf16[16,8192]{1,0:T(8,128)(2,1)}, f32[8,8192]{1,0:T(8,128)}) custom-call(s32[4]{0:T(128)} %lengths_ref.3, bf16[3,256,8192]{2,1,0:T(8,128)(2,1)} %bitcast.3, f32[3,3,8192]{2,1,0:T(4,128)} %taps_ref.3, f32[16,8192]{1,0:T(8,128)} %rate_ref.3, f32[16,256]{1,0:T(8,128)} %constant.11.clone.gather_ref), custom_call_target="tpu_custom_call" | custom-call | tf_op jit(solution)/shard_map/exchange/pallas_call | solution.py:417
  35.1 40.3 %output.1 = (bf16[256,8192]{1,0:T(8,128)(2,1)}, f32[256,128]{1,0:T(8,128)}) custom-call(s32[4]{0:T(128)} %lengths_ref.3, bf16[3,256,8192]{2,1,0:T(8,128)(2,1)} %bitcast.4, bf16[3,256,8192]{2,1,0:T(8,128)(2,1)} %bitcast.5, bf16[3,256,8192]{2,1,0:T(8,128)(2,1)} %bitcast.6, f32[8,8192]{1,0:T(8,128)} %get-tuple-element.8.edge_ref, f32[3,3,8192]{2,1,0:T(4,128)} %taps_ref.3, ...), custom_call_target="tpu_custom_call" | custom-call | tf_op jit(solution)/shard_map/output/pallas_call | solution.py:467

commit v3 on v2

--- a/solution.py
+++ b/solution.py
@@ -56,14 +56,16 @@
 
 def spread_matrix(rows):
     nodes = nodes_of(WIDE)
-    blocks = rows // BLOCK
-    index = np.arange(blocks * WIDE)
+    index = np.arange(rows // BLOCK * WIDE)
     group = index // WIDE
     place = np.arange(rows)[:, None]
-    end = np.where(group == blocks - 1, -1, (group + 1) * BLOCK - 1)[None, :]
-    used = (group == blocks - 1)[None, :] | (place // BLOCK == group[None, :] + 1)
-    lag = place - end
+    lag = place - ((group + 1) * BLOCK - 1)[None, :]
+    used = place // BLOCK == group[None, :] + 1
     return np.where(used, np.exp(-nodes[index % WIDE][None, :] * np.maximum(lag, 0)), 0.0)
+
+
+def entry_matrix(rows):
+    return np.exp(-nodes_of(WIDE)[None, :] * (np.arange(rows)[:, None] + 1.0))
 
 
 def near_matrices(rows):
@@ -100,27 +102,28 @@
     return jnp.concatenate([column] * (columns // column.shape[1]), axis=1)
 
 
-def fill_keeps(keep_ref, bounds):
+def fill_keeps(keep_ref, edge_keep_ref, bounds):
     rows = keep_ref.shape[1]
     place = lax.broadcasted_iota(jnp.int32, (rows, 128), 0)
     segment = seg_of(place, bounds)
     for i in range(2):
-        keep_ref[i] = (seg_of(place - (i + 1), bounds) == segment).astype(F32)
-
-
-def mix(block, edge, taps, keep_ref):
-    rows, columns = block.shape
+        keep = (seg_of(place - (i + 1), bounds) == segment).astype(F32)
+        keep_ref[i] = jnp.where(place > i, keep, 0.0)
+        edge_keep_ref[i] = jnp.where(place > i, 0.0, keep)[:8]
+
+
+def mix(block, edge, taps, keep_ref, edge_keep_ref):
+    columns = block.shape[1]
     now = block.astype(F32)
-    edge = edge.astype(F32)
-    row = lax.broadcasted_iota(jnp.int32, (rows, columns), 0)
-    one = jnp.where(row == 0, edge[1:2], pltpu.roll(now, 1, 0))
-    two = pltpu.roll(now, 2, 0)
-    two = jnp.where(row == 0, edge[0:1], jnp.where(row == 1, edge[1:2], two))
-    return (
+    mixed = (
         taps[0:1] * now
-        + taps[1:2] * (one * wide(keep_ref[0], columns))
-        + taps[2:3] * (two * wide(keep_ref[1], columns))
+        + taps[1:2] * (pltpu.roll(now, 1, 0) * wide(keep_ref[0], columns))
+        + taps[2:3] * (pltpu.roll(now, 2, 0) * wide(keep_ref[1], columns))
     )
+    row = lax.broadcasted_iota(jnp.int32, (8, columns), 0)
+    one = jnp.where(row == 0, edge[1:2], 0.0) * wide(edge_keep_ref[0], columns)
+    two = jnp.where(row == 0, edge[0:1], jnp.where(row == 1, edge[1:2], 0.0)) * wide(edge_keep_ref[1], columns)
+    return jnp.concatenate([mixed[:8] + (taps[1:2] * one + taps[2:3] * two), mixed[8:]], axis=0)
 
 
 def exchange_kernel(
@@ -128,11 +131,23 @@
     planes_ref,
     taps_ref,
     rate_ref,
+    residue_ref,
+    skip_ref,
     gather_ref,
+    spread_ref,
+    near_ref,
+    entry_ref,
+    edge_ref,
+    total_ref,
+    keep_ref,
+    edge_keep_ref,
+    matrix_ref,
+    gather_m,
+    spread_m,
+    near_m,
+    drive_ref,
+    weight_ref,
     arrived_ref,
-    edge_ref,
-    keep_ref,
-    matrix_ref,
     rows_ref,
     tail_ref,
     edge_send,
@@ -148,6 +163,7 @@
     local_sem,
     total_sem,
     back_sem,
+    out_sem,
 ):
     rows, channels = planes_ref.shape[1:]
     half = channels // 2
@@ -185,12 +201,25 @@
 
     bounds = bounds_of(lengths_ref, me * rows)
     zero_bounds = bounds_of(lengths_ref, 0)
-    fill_keeps(keep_ref, bounds)
-    place = lax.broadcasted_iota(jnp.int32, (WIDE, rows), 1)
-    same = seg_of(place, bounds) == seg_of(jnp.full((WIDE, rows), rows - 1, jnp.int32), bounds)
-    high, low = halves(jnp.where(same, gather_ref[...], 0.0))
-    matrix_ref[:WIDE] = high
-    matrix_ref[WIDE:] = low
+    fill_keeps(keep_ref, edge_keep_ref, bounds)
+    groups = gather_ref.shape[0]
+    place = lax.broadcasted_iota(jnp.int32, (groups, rows), 1)
+    end = lax.broadcasted_iota(jnp.int32, (groups, rows), 0) // WIDE * BLOCK + (BLOCK - 1)
+    high, low = halves(jnp.where(seg_of(place, bounds) == seg_of(end, bounds), gather_ref[...], 0.0))
+    gather_m[:groups] = high
+    gather_m[groups:] = low
+    matrix_ref[:WIDE] = high[groups - WIDE :]
+    matrix_ref[WIDE:] = low[groups - WIDE :]
+    place = lax.broadcasted_iota(jnp.int32, (rows, groups), 0)
+    end = lax.broadcasted_iota(jnp.int32, (rows, groups), 1) // WIDE * BLOCK + (BLOCK - 1)
+    high, low = halves(jnp.where(seg_of(place, bounds) == seg_of(end, bounds), spread_ref[...], 0.0))
+    spread_m[:, :groups] = high
+    spread_m[:, groups:] = low
+    across = lax.broadcasted_iota(jnp.int32, (rows, rows), 1)
+    down = lax.broadcasted_iota(jnp.int32, (rows, rows), 0)
+    same = seg_of(down, bounds) == seg_of(across, bounds)
+    for i in range(NEAR):
+        near_m[i] = jnp.where(same, near_ref[i].astype(F32), 0.0).astype(BF16)
     tail.wait()
     ends = [tail_ref[i].astype(F32)[14:16] for i in range(3)]
     packed = [e[:, :half] for e in ends] + [e[:, half:] for e in ends] + [jnp.zeros((4, half), F32)]
@@ -224,12 +253,18 @@
 
         def one_chunk(i, carry):
             here = pl.ds(pl.multiple_of(base + i * chunk, 128), chunk)
-            key = mix(rows_ref[0, :, here], edge_ref[2:4, here], taps_ref[:, 1, here], keep_ref)
-            value = mix(rows_ref[1, :, here], edge_ref[4:6, here], taps_ref[:, 2, here], keep_ref)
-            high, low = halves(key * value)
+            key = mix(rows_ref[0, :, here], edge_ref[2:4, here], taps_ref[:, 1, here], keep_ref, edge_keep_ref)
+            value = mix(rows_ref[1, :, here], edge_ref[4:6, here], taps_ref[:, 2, here], keep_ref, edge_keep_ref)
+            drive = key * value
+            drive_ref[:, here] = drive
+            high, low = halves(drive)
             moments = product_of(matrix_ref[...], high)
             moments = moments[:WIDE] + moments[WIDE:] + product_of(matrix_ref[:WIDE], low)
-            weights = lagrange(rate_ref[:, here], nodes_of(WIDE))
+            rate = rate_ref[:, here]
+            scale = residue_ref[:, here] * jnp.sqrt(1.0 - jnp.exp(-2.0 * rate))
+            weights = lagrange(rate, nodes_of(WIDE))
+            for n in range(WIDE):
+                weight_ref[n, :, here] = weights[n] * scale
             state = weights[0] * moments[0:1]
             for n in range(1, WIDE):
                 state = state + weights[n] * moments[n : n + 1]
@@ -245,6 +280,40 @@
 
     lax.fori_loop(1, TEAM, send_slice, 0)
     one_slice(0, local_land)
+
+    def out_copy(k):
+        return pltpu.make_async_copy(drive_ref.at[:, span(k)], total_ref.at[:, span(k)], out_sem.at[k])
+
+    def filter_slice(k, carry):
+        base = (rank + k) % TEAM * slim
+
+        def one_chunk(i, carry):
+            here = pl.ds(pl.multiple_of(base + i * chunk, 128), chunk)
+            rate = rate_ref[:, here]
+            scale = residue_ref[:, here] * jnp.sqrt(1.0 - jnp.exp(-2.0 * rate))
+            close = [jnp.sum(w * scale, axis=0, keepdims=True) for w in lagrange(rate, nodes_of(NEAR))]
+            share = jnp.concatenate(
+                [jnp.sum(weight_ref[n, :, here], axis=0, keepdims=True) for n in range(WIDE)], axis=0
+            )
+            drive = drive_ref[:, here]
+            high, low = halves(drive)
+            total = skip_ref[:, here] * drive
+            for n in range(NEAR):
+                total = total + close[n] * product_of(near_m[n], high)
+            moments = product_of(gather_m[...], high)
+            moments = moments[:groups] + moments[groups:] + product_of(gather_m[:groups], low)
+            moments = (moments.reshape(-1, WIDE, chunk) * share[None]).reshape(groups, chunk)
+            high, low = halves(moments)
+            total = total + product_of(spread_m[...], jnp.concatenate([high, high], axis=0))
+            total = total + product_of(spread_m[:, :groups], low)
+            drive_ref[:, here] = total
+            return carry
+
+        lax.fori_loop(0, slim // chunk, one_chunk, 0)
+        out_copy(k).start()
+        return carry
+
+    lax.fori_loop(0, 2, filter_slice, 0)
 
     mine = pl.ds(pl.multiple_of(rank * slim, 128), slim)
     rate = rate_ref[:, mine]
@@ -269,6 +338,7 @@
 
     for k in range(1, teams):
         total_copy(k).start()
+    lax.fori_loop(2, 5, filter_slice, 0)
     for k in range(1, teams):
         total_copy(k).wait()
     state = jnp.zeros(rate.shape, F32)
@@ -286,63 +356,54 @@
     for k in range(1, TEAM):
         back_copy(k).start()
     arrived_ref[:, mine] = back_send[rank]
+    lax.fori_loop(5, TEAM, filter_slice, 0)
     for k in range(1, TEAM):
         back_copy(k).wait()
     for k in range(1, TEAM):
         arrived_ref[:, span(TEAM - k)] = back_land[k]
 
+    def entry_chunk(i, carry):
+        here = pl.ds(pl.multiple_of(i * chunk, 128), chunk)
+        arrived = arrived_ref[:, here].astype(F32)
+        entry_ref[:, here] = jnp.concatenate(
+            [jnp.sum(weight_ref[n, :, here] * arrived, axis=0, keepdims=True) for n in range(WIDE)], axis=0
+        )
+        return carry
+
+    lax.fori_loop(0, channels // chunk, entry_chunk, 0)
+    for k in range(TEAM):
+        out_copy(k).wait()
+
 
 def output_kernel(
     fused,
     lengths_ref,
     query_ref,
-    key_ref,
-    value_ref,
+    total_ref,
     edge_ref,
     taps_ref,
-    rate_ref,
-    residue_ref,
-    skip_ref,
     gain_ref,
-    arrived_ref,
-    gather_ref,
-    spread_ref,
-    near_ref,
+    entry_ref,
+    arrive_ref,
     out_ref,
     square_ref,
     keep_ref,
-    gather_m,
-    spread_m,
-    near_m,
+    edge_keep_ref,
+    arrive_m,
     held_ref,
 ):
     rows, columns = query_ref.shape[1:]
     phase, step = pl.program_id(0), pl.program_id(1)
-    bounds = bounds_of(lengths_ref, lax.axis_index("ctx") * rows)
 
     @pl.when((phase == 0) & (step == 0))
     def _():
-        fill_keeps(keep_ref, bounds)
+        bounds = bounds_of(lengths_ref, lax.axis_index("ctx") * rows)
+        fill_keeps(keep_ref, edge_keep_ref, bounds)
         square_ref[...] = jnp.zeros_like(square_ref)
-        across = lax.broadcasted_iota(jnp.int32, (rows, rows), 1)
-        down = lax.broadcasted_iota(jnp.int32, (rows, rows), 0)
-        count = gather_ref.shape[0]
-        group = lax.broadcasted_iota(jnp.int32, (count, rows), 0) // WIDE
-        same = seg_of(lax.broadcasted_iota(jnp.int32, (count, rows), 1), bounds) == seg_of(
-            group * BLOCK + (BLOCK - 1), bounds
-        )
-        high, low = halves(jnp.where(same, gather_ref[...], 0.0))
-        gather_m[:count] = high
-        gather_m[count:] = low
-        group = lax.broadcasted_iota(jnp.int32, (rows, count), 1) // WIDE
-        end = jnp.where(group == rows // BLOCK - 1, -1, group * BLOCK + (BLOCK - 1))
-        same = seg_of(lax.broadcasted_iota(jnp.int32, (rows, count), 0), bounds) == seg_of(end, bounds)
-        high, low = halves(jnp.where(same, spread_ref[...], 0.0))
-        spread_m[:, :count] = high
-        spread_m[:, count:] = low
-        same = seg_of(down, bounds) == seg_of(across, bounds)
-        for i in range(NEAR):
-            near_m[i] = jnp.where(same, near_ref[i].astype(F32), 0.0).astype(BF16)
+        place = lax.broadcasted_iota(jnp.int32, (rows, WIDE), 0)
+        same = seg_of(place, bounds) == seg_of(jnp.full((rows, WIDE), -1, jnp.int32), bounds)
+        high, low = halves(jnp.where(same, arrive_ref[...], 0.0))
+        arrive_m[...] = jnp.concatenate([high, low, high], axis=1)
 
     @pl.when(phase == 0)
     def _():
@@ -350,29 +411,10 @@
 
         def one_chunk(index, carry):
             here = pl.ds(pl.multiple_of(index * chunk, 128), chunk)
-            product = mix(key_ref[0, :, here], edge_ref[2:4, here], taps_ref[:, 1, here], keep_ref) * mix(
-                value_ref[0, :, here], edge_ref[4:6, here], taps_ref[:, 2, here], keep_ref
-            )
-            rate = rate_ref[:, here]
-            scale = residue_ref[:, here] * jnp.sqrt(1.0 - jnp.exp(-2.0 * rate))
-            brought = scale * arrived_ref[:, here].astype(F32)
-            weights = lagrange(rate, nodes_of(WIDE))
-            share = jnp.concatenate([jnp.sum(w * scale, axis=0, keepdims=True) for w in weights], axis=0)
-            entry = jnp.concatenate([jnp.sum(w * brought, axis=0, keepdims=True) for w in weights], axis=0)
-            near = [jnp.sum(w * scale, axis=0, keepdims=True) for w in lagrange(rate, nodes_of(NEAR))]
-            high, low = halves(product)
-            total = skip_ref[:, here] * product
-            for i in range(NEAR):
-                total = total + near[i] * product_of(near_m[i], high)
-            count = gather_ref.shape[0]
-            moments = product_of(gather_m[...], high)
-            moments = moments[:count] + moments[count:] + product_of(gather_m[:count], low)
-            last = count - WIDE
-            moments = (moments[:last].reshape(-1, WIDE, chunk) * share[None]).reshape(last, chunk)
-            high, low = halves(jnp.concatenate([moments, entry], axis=0))
-            total = total + product_of(spread_m[...], jnp.concatenate([high, high], axis=0))
-            total = total + product_of(spread_m[:, :count], low)
-            response = mix(query_ref[0, :, here], edge_ref[0:2, here], taps_ref[:, 0, here], keep_ref) * total
+            high, low = halves(entry_ref[:, here])
+            total = total_ref[:, here] + product_of(arrive_m[...], jnp.concatenate([high, high, low], axis=0))
+            query = mix(query_ref[0, :, here], edge_ref[0:2, here], taps_ref[:, 0, here], keep_ref, edge_keep_ref)
+            response = query * total
             squares = response * response
             part = squares[:, :128]
             for i in range(1, chunk // 128):
@@ -409,22 +451,32 @@
     gather = jnp.asarray(gather_matrix(rows), F32)
     spread = jnp.asarray(spread_matrix(rows), F32)
     near = jnp.asarray(near_matrices(rows), BF16)
+    arrive = jnp.asarray(entry_matrix(rows), F32)
     smem = pl.BlockSpec(memory_space=pltpu.SMEM)
 
     vmem = pl.BlockSpec(memory_space=pltpu.VMEM)
     slim = channels // TEAM
     teams = count // TEAM
-    arrived, edge = pl.pallas_call(
+    groups = rows // BLOCK * WIDE
+    entry, edge, total = pl.pallas_call(
         exchange_kernel,
-        in_specs=[smem, pl.BlockSpec(memory_space=pl.ANY), vmem, vmem, vmem],
-        out_specs=[vmem, vmem],
+        in_specs=[smem, pl.BlockSpec(memory_space=pl.ANY)] + [vmem] * 7,
+        out_specs=[vmem, vmem, pl.BlockSpec(memory_space=pl.ANY)],
         out_shape=[
-            jax.ShapeDtypeStruct((poles, channels), BF16),
+            jax.ShapeDtypeStruct((WIDE, channels), F32),
             jax.ShapeDtypeStruct((8, channels), F32),
+            jax.ShapeDtypeStruct((rows, channels), F32),
         ],
         scratch_shapes=[
             pltpu.VMEM((2, rows, 128), F32),
+            pltpu.VMEM((2, 8, 128), F32),
             pltpu.VMEM((2 * WIDE, rows), BF16),
+            pltpu.VMEM((2 * groups, rows), BF16),
+            pltpu.VMEM((rows, 2 * groups), BF16),
+            pltpu.VMEM((NEAR, rows, rows), BF16),
+            pltpu.VMEM((rows, channels), F32),
+            pltpu.VMEM((WIDE, poles, channels), F32),
+            pltpu.VMEM((poles, channels), BF16),
             pltpu.VMEM((2, rows, channels), BF16),
             pltpu.VMEM((3, 16, channels), BF16),
             pltpu.VMEM((16, channels // 2), BF16),
@@ -440,12 +492,23 @@
             pltpu.SemaphoreType.DMA((TEAM, 2)),
             pltpu.SemaphoreType.DMA((teams, 2)),
             pltpu.SemaphoreType.DMA((TEAM, 2)),
+            pltpu.SemaphoreType.DMA((TEAM,)),
         ],
         compiler_params=pltpu.CompilerParams(
             collective_id=0, has_side_effects=True, vmem_limit_bytes=60 << 20
         ),
         name="exchange",
-    )(contig_lengths, planes, short_taps, decay_rate, jnp.asarray(gather_matrix(rows)[-WIDE:], F32))
+    )(
+        contig_lengths,
+        planes,
+        short_taps,
+        decay_rate,
+        residue,
+        skip_gain.reshape(1, channels),
+        gather,
+        spread,
+        near,
+    )
 
     def at(phase, j):
         return jnp.where(phase == 0, j, steps - 1)
@@ -470,18 +533,12 @@
         in_specs=[
             smem,
             plane_two(0),
-            plane_two(1),
-            plane_two(2),
+            per_block((rows, columns)),
             per_block((8, columns)),
             per_block((3, 3, columns)),
-            per_block((poles, columns)),
-            per_block((poles, columns)),
-            per_block((1, columns)),
             pl.BlockSpec((1, columns), lambda phase, j: (0, j)),
-            per_block((poles, columns)),
-            still(gather),
-            still(spread),
-            still(near),
+            per_block((WIDE, columns)),
+            still(arrive),
         ],
         out_specs=[pl.BlockSpec((rows, columns), out_map), pl.BlockSpec((rows, 128), lambda phase, j: (0, 0))],
         out_shape=[
@@ -490,29 +547,13 @@
         ],
         scratch_shapes=[
             pltpu.VMEM((2, rows, 128), F32),
-            pltpu.VMEM((2 * gather.shape[0], rows), BF16),
-            pltpu.VMEM((rows, 2 * spread.shape[1]), BF16),
-            pltpu.VMEM(near.shape, BF16),
+            pltpu.VMEM((2, 8, 128), F32),
+            pltpu.VMEM((rows, 3 * WIDE), BF16),
             pltpu.VMEM((steps, rows, columns) if fused else (1, 8, 128), F32),
         ],
         compiler_params=pltpu.CompilerParams(vmem_limit_bytes=60 << 20),
         name="output",
-    )(
-        contig_lengths,
-        planes,
-        planes,
-        planes,
-        edge,
-        short_taps,
-        decay_rate,
-        residue,
-        skip_gain.reshape(1, channels),
-        norm_gain.reshape(1, channels),
-        arrived,
-        gather,
-        spread,
-        near,
-    )
+    )(contig_lengths, planes, total, edge, short_taps, norm_gain.reshape(1, channels), entry, arrive)
     if fused:
         return result
     mean = lax.psum(jnp.sum(squares, axis=1, keepdims=True), "chan") / D

time: 75.8 us -> 70.5 us (0.930)
  Pallas kernels: 75.4 us -> 70 us
    pallas_call x1, Pallas kernels: 40.3 us -> 16 us  [shards(): pl.pallas_call(functools.partial(output_kernel, fused), grid=(2 if fused...]
    pallas_call x1, Pallas kernels: 35.1 us -> 53.9 us  [shards(): pl.pallas_call(exchange_kernel, in_specs=[smem, pl.BlockSpec(memory_space...]
where the time goes in v3:
time: 70.5 us; the launch traced here: 70 us
  Pallas kernels  70 us (99%)
    pallas_call x1, Pallas kernels, shards(): pl.pallas_call(exchange_kernel, in_specs=[smem, pl.BlockSpec(memory_space...  53.9 us
    pallas_call x1, Pallas kernels, shards(): pl.pallas_call(functools.partial(output_kernel, fused), grid=(2 if fused...  16 us

profile of v3, /device:TPU:0, one launch (start us, length us, event | category | flops | bytes accessed | tf_op | source)
XLA Modules:
  0.0 70.0 jit_solution(7949769195518604738)
XLA Ops:
  0.0 53.9 %exchange.1 = (f32[16,8192]{1,0:T(8,128)}, f32[8,8192]{1,0:T(8,128)}, f32[256,8192]{1,0:T(8,128)}) custom-call(s32[4]{0:T(128)} %lengths_ref.3, bf16[3,256,8192]{2,1,0:T(8,128)(2,1)} %bitcast.3, f32[3,3,8192]{2,1,0:T(4,128)} %taps_ref.3, f32[16,8192]{1,0:T(8,128)} %rate_ref.1, f32[16,8192]{1,0:T(8,128)} %residue_ref.1, f32[1,8192]{1,0:T(1,128)} %bitcast.5, ...), custom_call_target="tpu_custom_call" | custom-call | tf_op jit(solution)/shard_map/exchange/pallas_call | solution.py:461
  54.0 16.0 %output.1 = (bf16[256,8192]{1,0:T(8,128)(2,1)}, f32[256,128]{1,0:T(8,128)}) custom-call(s32[4]{0:T(128)} %lengths_ref.3, bf16[3,256,8192]{2,1,0:T(8,128)(2,1)} %bitcast.4, f32[256,8192]{1,0:T(8,128)} %get-tuple-element.9.total_ref, f32[8,8192]{1,0:T(8,128)} %get-tuple-element.10.edge_ref, f32[3,3,8192]{2,1,0:T(4,128)} %taps_ref.3, f32[1,8192]{1,0:T(1,128)} %bitcast.6, ...), custom_call_target="tpu_custom_call" | custom-call | tf_op jit(solution)/shard_map/output/pallas_call | solution.py:530

commit v4 on v3

--- a/solution.py
+++ b/solution.py
@@ -2,6 +2,7 @@
 
 import jax
 import jax.numpy as jnp
+import ml_dtypes
 import numpy as np
 from jax import lax
 from jax.experimental import pallas as pl
@@ -13,8 +14,10 @@
 RATE_TOP = 1.0 / 30.0 * (1.0 + 1e-6)
 BLOCK = 32
 WIDE = 16
-NEAR = 7
+NEAR = 6
+MIDDLE = (BLOCK - 1) / 2
 TEAM = 8
+LEAD = 16
 CHUNK = 256
 F32 = jnp.float32
 BF16 = jnp.bfloat16
@@ -46,22 +49,26 @@
     return weights
 
 
+def split(matrix):
+    high = matrix.astype(ml_dtypes.bfloat16)
+    return high, (matrix - high.astype(np.float64)).astype(ml_dtypes.bfloat16)
+
+
 def gather_matrix(rows):
     nodes = nodes_of(WIDE)
     index = np.arange(rows // BLOCK * WIDE)
     end = (index // WIDE + 1) * BLOCK - 1
     lag = end[:, None] - np.arange(rows)[None, :]
-    return np.where(lag >= 0, np.exp(-nodes[index % WIDE][:, None] * np.maximum(lag, 0)), 0.0)
-
-
-def spread_matrix(rows):
-    nodes = nodes_of(WIDE)
-    index = np.arange(rows // BLOCK * WIDE)
-    group = index // WIDE
-    place = np.arange(rows)[:, None]
-    lag = place - ((group + 1) * BLOCK - 1)[None, :]
-    used = place // BLOCK == group[None, :] + 1
-    return np.where(used, np.exp(-nodes[index % WIDE][None, :] * np.maximum(lag, 0)), 0.0)
+    matrix = np.where(lag >= 0, np.exp(-nodes[index % WIDE][:, None] * np.maximum(lag, 0)), 0.0)
+    return np.concatenate(split(matrix), axis=0)
+
+
+def block_matrix(rows):
+    place = np.arange(rows)[:, None] % BLOCK
+    lag = place - np.arange(BLOCK)[None, :]
+    near = [np.where(lag >= 0, np.exp(-node * (lag - MIDDLE)), 0.0) for node in nodes_of(NEAR)]
+    high, low = split(np.exp(-nodes_of(WIDE)[None, :] * (place + 1.0)))
+    return np.concatenate([split(n)[0] for n in near] + [high, low, high], axis=1)
 
 
 def entry_matrix(rows):
@@ -102,28 +109,24 @@
     return jnp.concatenate([column] * (columns // column.shape[1]), axis=1)
 
 
-def fill_keeps(keep_ref, edge_keep_ref, bounds):
-    rows = keep_ref.shape[1]
-    place = lax.broadcasted_iota(jnp.int32, (rows, 128), 0)
-    segment = seg_of(place, bounds)
-    for i in range(2):
-        keep = (seg_of(place - (i + 1), bounds) == segment).astype(F32)
-        keep_ref[i] = jnp.where(place > i, keep, 0.0)
-        edge_keep_ref[i] = jnp.where(place > i, 0.0, keep)[:8]
-
-
-def mix(block, edge, taps, keep_ref, edge_keep_ref):
-    columns = block.shape[1]
-    now = block.astype(F32)
-    mixed = (
-        taps[0:1] * now
-        + taps[1:2] * (pltpu.roll(now, 1, 0) * wide(keep_ref[0], columns))
-        + taps[2:3] * (pltpu.roll(now, 2, 0) * wide(keep_ref[1], columns))
-    )
-    row = lax.broadcasted_iota(jnp.int32, (8, columns), 0)
-    one = jnp.where(row == 0, edge[1:2], 0.0) * wide(edge_keep_ref[0], columns)
-    two = jnp.where(row == 0, edge[0:1], jnp.where(row == 1, edge[1:2], 0.0)) * wide(edge_keep_ref[1], columns)
-    return jnp.concatenate([mixed[:8] + (taps[1:2] * one + taps[2:3] * two), mixed[8:]], axis=0)
+def shift_shape(rows):
+    return (2 * rows, BLOCK + LEAD)
+
+
+def fill_shifts(shift_ref, bounds):
+    down = lax.broadcasted_iota(jnp.int32, shift_ref.shape, 0)
+    column = lax.broadcasted_iota(jnp.int32, shift_ref.shape, 1)
+    by = 1 + down % (2 * BLOCK) // BLOCK
+    place = down // (2 * BLOCK) * BLOCK + down % BLOCK
+    same = seg_of(place, bounds) == seg_of(place - by, bounds)
+    used = same & (column == LEAD + down % BLOCK - by)
+    shift_ref[...] = jnp.where(used, 1.0, 0.0).astype(BF16)
+
+
+def mix(block, taps, shifts):
+    moved = product_of(shifts, block)
+    now = block[LEAD:].astype(F32)
+    return taps[0:1] * now + taps[1:2] * moved[:BLOCK] + taps[2:3] * moved[BLOCK:]
 
 
 def exchange_kernel(
@@ -134,17 +137,14 @@
     residue_ref,
     skip_ref,
     gather_ref,
-    spread_ref,
-    near_ref,
+    block_ref,
     entry_ref,
     edge_ref,
     total_ref,
-    keep_ref,
-    edge_keep_ref,
+    shift_ref,
     matrix_ref,
     gather_m,
-    spread_m,
-    near_m,
+    block_m,
     drive_ref,
     weight_ref,
     arrived_ref,
@@ -185,7 +185,7 @@
 
     def load(k):
         return pltpu.make_async_copy(
-            planes_ref.at[pl.ds(1, 2), :, span(k)], rows_ref.at[:, :, span(k)], rows_sem.at[k]
+            planes_ref.at[pl.ds(1, 2), :, span(k)], rows_ref.at[:, pl.ds(LEAD, rows), span(k)], rows_sem.at[k]
         )
 
     tail = pltpu.make_async_copy(planes_ref.at[:, pl.ds(rows - 16, 16), :], tail_ref, tail_sem)
@@ -201,25 +201,20 @@
 
     bounds = bounds_of(lengths_ref, me * rows)
     zero_bounds = bounds_of(lengths_ref, 0)
-    fill_keeps(keep_ref, edge_keep_ref, bounds)
-    groups = gather_ref.shape[0]
-    place = lax.broadcasted_iota(jnp.int32, (groups, rows), 1)
-    end = lax.broadcasted_iota(jnp.int32, (groups, rows), 0) // WIDE * BLOCK + (BLOCK - 1)
-    high, low = halves(jnp.where(seg_of(place, bounds) == seg_of(end, bounds), gather_ref[...], 0.0))
-    gather_m[:groups] = high
-    gather_m[groups:] = low
-    matrix_ref[:WIDE] = high[groups - WIDE :]
-    matrix_ref[WIDE:] = low[groups - WIDE :]
-    place = lax.broadcasted_iota(jnp.int32, (rows, groups), 0)
-    end = lax.broadcasted_iota(jnp.int32, (rows, groups), 1) // WIDE * BLOCK + (BLOCK - 1)
-    high, low = halves(jnp.where(seg_of(place, bounds) == seg_of(end, bounds), spread_ref[...], 0.0))
-    spread_m[:, :groups] = high
-    spread_m[:, groups:] = low
-    across = lax.broadcasted_iota(jnp.int32, (rows, rows), 1)
-    down = lax.broadcasted_iota(jnp.int32, (rows, rows), 0)
-    same = seg_of(down, bounds) == seg_of(across, bounds)
-    for i in range(NEAR):
-        near_m[i] = jnp.where(same, near_ref[i].astype(F32), 0.0).astype(BF16)
+    fill_shifts(shift_ref, bounds)
+    groups = gather_ref.shape[0] // 2
+    place = lax.broadcasted_iota(jnp.int32, (2 * groups, rows), 1)
+    end = lax.broadcasted_iota(jnp.int32, (2 * groups, rows), 0) % groups // WIDE * BLOCK + (BLOCK - 1)
+    kept = jnp.where(seg_of(place, bounds) == seg_of(end, bounds), gather_ref[...].astype(F32), 0.0).astype(BF16)
+    gather_m[...] = kept
+    matrix_ref[:WIDE] = kept[groups - WIDE : groups]
+    matrix_ref[WIDE:] = kept[2 * groups - WIDE :]
+    place = lax.broadcasted_iota(jnp.int32, block_ref.shape, 0)
+    start = place // BLOCK * BLOCK
+    column = lax.broadcasted_iota(jnp.int32, block_ref.shape, 1)
+    source = jnp.where(column < NEAR * BLOCK, start + column % BLOCK, start - 1)
+    same = seg_of(place, bounds) == seg_of(source, bounds)
+    block_m[...] = jnp.where(same, block_ref[...].astype(F32), 0.0).astype(BF16)
     tail.wait()
     ends = [tail_ref[i].astype(F32)[14:16] for i in range(3)]
     packed = [e[:, :half] for e in ends] + [e[:, half:] for e in ends] + [jnp.zeros((4, half), F32)]
@@ -240,9 +235,16 @@
     edge_copy.start()
     edge_copy.wait()
     landed = jnp.where(me == 0, 0.0, edge_land[...].astype(F32))
-    blank = jnp.zeros((2, half), F32)
-    edge_ref[:, :half] = jnp.concatenate([landed[0:6], blank], axis=0)
-    edge_ref[:, half:] = jnp.concatenate([landed[6:12], blank], axis=0)
+    blank = jnp.zeros((LEAD - 2, half), F32)
+    for side in range(2):
+        there = slice(side * half, (side + 1) * half)
+        for i in range(3):
+            first = 6 * side + 2 * i
+            lead = jnp.concatenate([blank, landed[first : first + 2]], axis=0).astype(BF16)
+            if i == 0:
+                edge_ref[:, there] = lead
+            else:
+                rows_ref[i - 1, :LEAD, there] = lead
 
     def local_copy(k):
         return remote(local_send.at[k], local_land.at[k], (local_sem.at[k, 0], local_sem.at[k, 1]), mate(k))
@@ -253,13 +255,17 @@
 
         def one_chunk(i, carry):
             here = pl.ds(pl.multiple_of(base + i * chunk, 128), chunk)
-            key = mix(rows_ref[0, :, here], edge_ref[2:4, here], taps_ref[:, 1, here], keep_ref, edge_keep_ref)
-            value = mix(rows_ref[1, :, here], edge_ref[4:6, here], taps_ref[:, 2, here], keep_ref, edge_keep_ref)
-            drive = key * value
-            drive_ref[:, here] = drive
-            high, low = halves(drive)
-            moments = product_of(matrix_ref[...], high)
-            moments = moments[:WIDE] + moments[WIDE:] + product_of(matrix_ref[:WIDE], low)
+            rounded = []
+            for b in range(rows // BLOCK):
+                with_lead = slice(b * BLOCK, (b + 1) * BLOCK + LEAD)
+                shifts = shift_ref[2 * b * BLOCK : 2 * (b + 1) * BLOCK, :]
+                drive = mix(rows_ref[0, with_lead, here], taps_ref[:, 1, here], shifts) * mix(
+                    rows_ref[1, with_lead, here], taps_ref[:, 2, here], shifts
+                )
+                drive_ref[b * BLOCK : (b + 1) * BLOCK, here] = drive
+                rounded.append(drive.astype(BF16))
+            moments = product_of(matrix_ref[...], jnp.concatenate(rounded, axis=0))
+            moments = moments[:WIDE] + moments[WIDE:]
             rate = rate_ref[:, here]
             scale = residue_ref[:, here] * jnp.sqrt(1.0 - jnp.exp(-2.0 * rate))
             weights = lagrange(rate, nodes_of(WIDE))
@@ -268,7 +274,7 @@
             state = weights[0] * moments[0:1]
             for n in range(1, WIDE):
                 state = state + weights[n] * moments[n : n + 1]
-            into[k, :, pl.ds(pl.multiple_of(i * chunk, 128), chunk)] = state.astype(BF16)
+            into[k, :, pl.ds(pl.multiple_of(i * chunk, 128), chunk)] = state
             return carry
 
         lax.fori_loop(0, slim // chunk, one_chunk, 0)
@@ -291,22 +297,27 @@
             here = pl.ds(pl.multiple_of(base + i * chunk, 128), chunk)
             rate = rate_ref[:, here]
             scale = residue_ref[:, here] * jnp.sqrt(1.0 - jnp.exp(-2.0 * rate))
+            scale = scale * jnp.exp(F32(-MIDDLE) * rate)
             close = [jnp.sum(w * scale, axis=0, keepdims=True) for w in lagrange(rate, nodes_of(NEAR))]
             share = jnp.concatenate(
                 [jnp.sum(weight_ref[n, :, here], axis=0, keepdims=True) for n in range(WIDE)], axis=0
             )
-            drive = drive_ref[:, here]
-            high, low = halves(drive)
-            total = skip_ref[:, here] * drive
-            for n in range(NEAR):
-                total = total + close[n] * product_of(near_m[n], high)
-            moments = product_of(gather_m[...], high)
-            moments = moments[:groups] + moments[groups:] + product_of(gather_m[:groups], low)
+            skip = skip_ref[:, here]
+            moments = product_of(gather_m[...], drive_ref[:, here].astype(BF16))
+            moments = moments[:groups] + moments[groups:]
             moments = (moments.reshape(-1, WIDE, chunk) * share[None]).reshape(groups, chunk)
             high, low = halves(moments)
-            total = total + product_of(spread_m[...], jnp.concatenate([high, high], axis=0))
-            total = total + product_of(spread_m[:, :groups], low)
-            drive_ref[:, here] = total
+            for b in range(rows // BLOCK):
+                span_b = slice(b * BLOCK, (b + 1) * BLOCK)
+                drive = drive_ref[span_b, here]
+                parts = [(c * drive).astype(BF16) for c in close]
+                if b > 0:
+                    before = slice((b - 1) * WIDE, b * WIDE)
+                    parts += [high[before], high[before], low[before]]
+                    weights = block_m[span_b, :]
+                else:
+                    weights = block_m[span_b, : NEAR * BLOCK]
+                drive_ref[span_b, here] = skip * drive + product_of(weights, jnp.concatenate(parts, axis=0))
             return carry
 
         lax.fori_loop(0, slim // chunk, one_chunk, 0)
@@ -327,11 +338,11 @@
 
     for k in range(1, TEAM):
         local_copy(k).wait()
-    local = [local_land[(rank + TEAM - s) % TEAM].astype(F32) for s in range(TEAM)]
+    local = [local_land[(rank + TEAM - s) % TEAM] for s in range(TEAM)]
     total = local[0]
     for s in range(1, TEAM):
         total = total * (fade * whole(team * TEAM + s, 1)) + local[s]
-    total_land[0] = total.astype(BF16)
+    total_land[0] = total
 
     def total_copy(k):
         return remote(total_land.at[0], total_land.at[k], (total_sem.at[k, 0], total_sem.at[k, 1]), peer(k))
@@ -343,10 +354,10 @@
         total_copy(k).wait()
     state = jnp.zeros(rate.shape, F32)
     for g in range(teams - 1):
-        after = state * (fade_team * whole(g * TEAM, TEAM)) + total_land[(team + teams - g) % teams].astype(F32)
+        after = state * (fade_team * whole(g * TEAM, TEAM)) + total_land[(team + teams - g) % teams]
         state = jnp.where(g < team, after, state)
     for s in range(TEAM):
-        back_send[s] = state.astype(BF16)
+        back_send[s] = state
         if s < TEAM - 1:
             state = state * (fade * whole(team * TEAM + s, 1)) + local[s]
 
@@ -364,7 +375,7 @@
 
     def entry_chunk(i, carry):
         here = pl.ds(pl.multiple_of(i * chunk, 128), chunk)
-        arrived = arrived_ref[:, here].astype(F32)
+        arrived = arrived_ref[:, here]
         entry_ref[:, here] = jnp.concatenate(
             [jnp.sum(weight_ref[n, :, here] * arrived, axis=0, keepdims=True) for n in range(WIDE)], axis=0
         )
@@ -387,8 +398,7 @@
     arrive_ref,
     out_ref,
     square_ref,
-    keep_ref,
-    edge_keep_ref,
+    shift_ref,
     arrive_m,
     held_ref,
 ):
@@ -398,7 +408,7 @@
     @pl.when((phase == 0) & (step == 0))
     def _():
         bounds = bounds_of(lengths_ref, lax.axis_index("ctx") * rows)
-        fill_keeps(keep_ref, edge_keep_ref, bounds)
+        fill_shifts(shift_ref, bounds)
         square_ref[...] = jnp.zeros_like(square_ref)
         place = lax.broadcasted_iota(jnp.int32, (rows, WIDE), 0)
         same = seg_of(place, bounds) == seg_of(jnp.full((rows, WIDE), -1, jnp.int32), bounds)
@@ -412,18 +422,25 @@
         def one_chunk(index, carry):
             here = pl.ds(pl.multiple_of(index * chunk, 128), chunk)
             high, low = halves(entry_ref[:, here])
-            total = total_ref[:, here] + product_of(arrive_m[...], jnp.concatenate([high, high, low], axis=0))
-            query = mix(query_ref[0, :, here], edge_ref[0:2, here], taps_ref[:, 0, here], keep_ref, edge_keep_ref)
-            response = query * total
-            squares = response * response
-            part = squares[:, :128]
-            for i in range(1, chunk // 128):
-                part = part + squares[:, i * 128 : (i + 1) * 128]
-            square_ref[...] += part
-            if fused:
-                held_ref[step, :, here] = response
-            else:
-                out_ref[:, here] = response
+            entry = jnp.concatenate([high, high, low], axis=0)
+            taps = taps_ref[:, 0, here]
+            for b in range(rows // BLOCK):
+                span_b = slice(b * BLOCK, (b + 1) * BLOCK)
+                if b == 0:
+                    block = jnp.concatenate([edge_ref[:, here], query_ref[0, span_b, here]], axis=0)
+                else:
+                    block = query_ref[0, b * BLOCK - LEAD : (b + 1) * BLOCK, here]
+                query = mix(block, taps, shift_ref[2 * b * BLOCK : 2 * (b + 1) * BLOCK, :])
+                response = query * (total_ref[span_b, here] + product_of(arrive_m[span_b, :], entry))
+                squares = response * response
+                part = squares[:, :128]
+                for i in range(1, chunk // 128):
+                    part = part + squares[:, i * 128 : (i + 1) * 128]
+                square_ref[span_b, :] += part
+                if fused:
+                    held_ref[step, span_b, here] = response
+                else:
+                    out_ref[span_b, here] = response
             return carry
 
         lax.fori_loop(0, columns // chunk, one_chunk, 0)
@@ -437,7 +454,12 @@
 
         @pl.when(phase == 1)
         def _():
-            out_ref[...] = (held_ref[step] * wide(square_ref[...], columns) * gain_ref[...]).astype(BF16)
+            for b in range(rows // BLOCK):
+                span_b = slice(b * BLOCK, (b + 1) * BLOCK)
+                scale = square_ref[span_b, :]
+                for i in range(columns // 128):
+                    here = slice(i * 128, (i + 1) * 128)
+                    out_ref[span_b, here] = (held_ref[step, span_b, here] * scale * gain_ref[:, here]).astype(BF16)
 
 
 def shards(features, short_taps, decay_rate, residue, skip_gain, norm_gain, contig_lengths):
@@ -448,44 +470,40 @@
     planes = jnp.transpose(features, (1, 0, 2))
     columns = min(1024, channels)
     steps = channels // columns
-    gather = jnp.asarray(gather_matrix(rows), F32)
-    spread = jnp.asarray(spread_matrix(rows), F32)
-    near = jnp.asarray(near_matrices(rows), BF16)
+    gather = jnp.asarray(gather_matrix(rows))
+    block = jnp.asarray(block_matrix(rows))
     arrive = jnp.asarray(entry_matrix(rows), F32)
     smem = pl.BlockSpec(memory_space=pltpu.SMEM)
 
     vmem = pl.BlockSpec(memory_space=pltpu.VMEM)
     slim = channels // TEAM
     teams = count // TEAM
-    groups = rows // BLOCK * WIDE
     entry, edge, total = pl.pallas_call(
         exchange_kernel,
-        in_specs=[smem, pl.BlockSpec(memory_space=pl.ANY)] + [vmem] * 7,
+        in_specs=[smem, pl.BlockSpec(memory_space=pl.ANY)] + [vmem] * 6,
         out_specs=[vmem, vmem, pl.BlockSpec(memory_space=pl.ANY)],
         out_shape=[
             jax.ShapeDtypeStruct((WIDE, channels), F32),
-            jax.ShapeDtypeStruct((8, channels), F32),
+            jax.ShapeDtypeStruct((LEAD, channels), BF16),
             jax.ShapeDtypeStruct((rows, channels), F32),
         ],
         scratch_shapes=[
-            pltpu.VMEM((2, rows, 128), F32),
-            pltpu.VMEM((2, 8, 128), F32),
+            pltpu.VMEM(shift_shape(rows), BF16),
             pltpu.VMEM((2 * WIDE, rows), BF16),
-            pltpu.VMEM((2 * groups, rows), BF16),
-            pltpu.VMEM((rows, 2 * groups), BF16),
-            pltpu.VMEM((NEAR, rows, rows), BF16),
+            pltpu.VMEM(gather.shape, BF16),
+            pltpu.VMEM(block.shape, BF16),
             pltpu.VMEM((rows, channels), F32),
             pltpu.VMEM((WIDE, poles, channels), F32),
-            pltpu.VMEM((poles, channels), BF16),
-            pltpu.VMEM((2, rows, channels), BF16),
+            pltpu.VMEM((poles, channels), F32),
+            pltpu.VMEM((2, LEAD + rows, channels), BF16),
             pltpu.VMEM((3, 16, channels), BF16),
             pltpu.VMEM((16, channels // 2), BF16),
             pltpu.VMEM((16, channels // 2), BF16),
-            pltpu.VMEM((TEAM, poles, slim), BF16),
-            pltpu.VMEM((TEAM, poles, slim), BF16),
-            pltpu.VMEM((teams, poles, slim), BF16),
-            pltpu.VMEM((TEAM, poles, slim), BF16),
-            pltpu.VMEM((TEAM, poles, slim), BF16),
+            pltpu.VMEM((TEAM, poles, slim), F32),
+            pltpu.VMEM((TEAM, poles, slim), F32),
+            pltpu.VMEM((teams, poles, slim), F32),
+            pltpu.VMEM((TEAM, poles, slim), F32),
+            pltpu.VMEM((TEAM, poles, slim), F32),
             pltpu.SemaphoreType.DMA((TEAM,)),
             pltpu.SemaphoreType.DMA,
             pltpu.SemaphoreType.DMA((2,)),
@@ -506,8 +524,7 @@
         residue,
         skip_gain.reshape(1, channels),
         gather,
-        spread,
-        near,
+        block,
     )
 
     def at(phase, j):
@@ -534,7 +551,7 @@
             smem,
             plane_two(0),
             per_block((rows, columns)),
-            per_block((8, columns)),
+            per_block((LEAD, columns)),
             per_block((3, 3, columns)),
             pl.BlockSpec((1, columns), lambda phase, j: (0, j)),
             per_block((WIDE, columns)),
@@ -546,8 +563,7 @@
             jax.ShapeDtypeStruct((rows, 128), F32),
         ],
         scratch_shapes=[
-            pltpu.VMEM((2, rows, 128), F32),
-            pltpu.VMEM((2, 8, 128), F32),
+            pltpu.VMEM(shift_shape(rows), BF16),
             pltpu.VMEM((rows, 3 * WIDE), BF16),
             pltpu.VMEM((steps, rows, columns) if fused else (1, 8, 128), F32),
         ],

time: 70.5 us -> 61.1 us (0.87)
  Pallas kernels: 70 us -> 60.5 us
    pallas_call x1, Pallas kernels: 53.9 us -> 43.6 us  [shards(): pl.pallas_call(exchange_kernel, in_specs=[smem, pl.BlockSpec(memory_space...]
    pallas_call x1, Pallas kernels: 16 us -> 17 us  [shards(): pl.pallas_call(functools.partial(output_kernel, fused), grid=(2 if fused...]
where the time goes in v4:
time: 61.1 us; the launch traced here: 60.6 us
  Pallas kernels  60.5 us (99%)
    pallas_call x1, Pallas kernels, shards(): pl.pallas_call(exchange_kernel, in_specs=[smem, pl.BlockSpec(memory_space...  43.6 us
    pallas_call x1, Pallas kernels, shards(): pl.pallas_call(functools.partial(output_kernel, fused), grid=(2 if fused...  17 us

profile of v4, /device:TPU:0, one launch (start us, length us, event | category | flops | bytes accessed | tf_op | source)
XLA Modules:
  0.0 60.6 jit_solution(11786287902509833443)
XLA Ops:
  0.0 43.6 %exchange.1 = (f32[16,8192]{1,0:T(8,128)}, bf16[16,8192]{1,0:T(8,128)(2,1)}, f32[256,8192]{1,0:T(8,128)}) custom-call(s32[4]{0:T(128)} %lengths_ref.3, bf16[3,256,8192]{2,1,0:T(8,128)(2,1)} %bitcast.3, f32[3,3,8192]{2,1,0:T(4,128)} %taps_ref.3, f32[16,8192]{1,0:T(8,128)} %rate_ref.1, f32[16,8192]{1,0:T(8,128)} %residue_ref.1, f32[1,8192]{1,0:T(1,128)} %bitcast.5, ...), custom_call_target="tpu_custom_call" | custom-call | tf_op jit(solution)/shard_map/exchange/pallas_call | solution.py:481
  43.6 17.0 %output.1 = (bf16[256,8192]{1,0:T(8,128)(2,1)}, f32[256,128]{1,0:T(8,128)}) custom-call(s32[4]{0:T(128)} %lengths_ref.3, bf16[3,256,8192]{2,1,0:T(8,128)(2,1)} %bitcast.4, f32[256,8192]{1,0:T(8,128)} %get-tuple-element.9.total_ref, bf16[16,8192]{1,0:T(8,128)(2,1)} %get-tuple-element.10.edge_ref, f32[3,3,8192]{2,1,0:T(4,128)} %taps_ref.3, f32[1,8192]{1,0:T(1,128)} %bitcast.6, ...), custom_call_target="tpu_custom_call" | custom-call | tf_op jit(solution)/shard_map/output/pallas_call | solution.py:547

commit v5 on v4

--- a/solution.py
+++ b/solution.py
@@ -18,7 +18,7 @@
 MIDDLE = (BLOCK - 1) / 2
 TEAM = 8
 LEAD = 16
-CHUNK = 256
+CHUNK = 512
 F32 = jnp.float32
 BF16 = jnp.bfloat16
 
@@ -468,7 +468,7 @@
     fused = lax.axis_size("chan") == 1
     poles = decay_rate.shape[0]
     planes = jnp.transpose(features, (1, 0, 2))
-    columns = min(1024, channels)
+    columns = min(2048, channels)
     steps = channels // columns
     gather = jnp.asarray(gather_matrix(rows))
     block = jnp.asarray(block_matrix(rows))

time: 61.1 us -> 52.3 us (0.86)
  the two profiles are of different devices: /device:TPU:0 before, /device:TPU:13 now
where the time goes in v5:
time: 52.3 us; the launch traced here: 52 us
  Pallas kernels  52 us (99%)
    pallas_call x1, Pallas kernels, shards(): pl.pallas_call(exchange_kernel, in_specs=[smem, pl.BlockSpec(memory_space...  39.2 us
    pallas_call x1, Pallas kernels, shards(): pl.pallas_call(functools.partial(output_kernel, fused), grid=(2 if fused...  12.9 us

profile of v5, /device:TPU:13, one launch (start us, length us, event | category | flops | bytes accessed | tf_op | source)
XLA Modules:
  0.0 52.0 jit_solution(15237646884375693163)
XLA Ops:
  0.0 39.2 %exchange.1 = (f32[16,8192]{1,0:T(8,128)}, bf16[16,8192]{1,0:T(8,128)(2,1)}, f32[256,8192]{1,0:T(8,128)}) custom-call(s32[4]{0:T(128)} %lengths_ref.3, bf16[3,256,8192]{2,1,0:T(8,128)(2,1)} %bitcast.3, f32[3,3,8192]{2,1,0:T(4,128)} %taps_ref.3, f32[16,8192]{1,0:T(8,128)} %rate_ref.1, f32[16,8192]{1,0:T(8,128)} %residue_ref.1, f32[1,8192]{1,0:T(1,128)} %bitcast.5, ...), custom_call_target="tpu_custom_call" | custom-call | tf_op jit(solution)/shard_map/exchange/pallas_call | solution.py:481
  39.2 12.9 %output.1 = (bf16[256,8192]{1,0:T(8,128)(2,1)}, f32[256,128]{1,0:T(8,128)}) custom-call(s32[4]{0:T(128)} %lengths_ref.3, bf16[3,256,8192]{2,1,0:T(8,128)(2,1)} %bitcast.4, f32[256,8192]{1,0:T(8,128)} %get-tuple-element.9.total_ref, bf16[16,8192]{1,0:T(8,128)(2,1)} %get-tuple-element.10.edge_ref, f32[3,3,8192]{2,1,0:T(4,128)} %taps_ref.3, f32[1,8192]{1,0:T(1,128)} %bitcast.6, ...), custom_call_target="tpu_custom_call" | custom-call | tf_op jit(solution)/shard_map/output/pallas_call | solution.py:547

commit v6 on v5

--- a/solution.py
+++ b/solution.py
@@ -18,7 +18,7 @@
 MIDDLE = (BLOCK - 1) / 2
 TEAM = 8
 LEAD = 16
-CHUNK = 512
+CHUNK = 1024
 F32 = jnp.float32
 BF16 = jnp.bfloat16
 

time: 52.3 us -> 49.9 us (0.954)
  the two profiles are of different devices: /device:TPU:13 before, /device:TPU:5 now
where the time goes in v6:
time: 49.9 us; the launch traced here: 49.7 us
  Pallas kernels  49.7 us (100%)
    pallas_call x1, Pallas kernels, shards(): pl.pallas_call(exchange_kernel, in_specs=[smem, pl.BlockSpec(memory_space...  37.6 us
    pallas_call x1, Pallas kernels, shards(): pl.pallas_call(functools.partial(output_kernel, fused), grid=(2 if fused...  12.1 us

profile of v6, /device:TPU:5, one launch (start us, length us, event | category | flops | bytes accessed | tf_op | source)
XLA Modules:
  0.0 49.7 jit_solution(10079007839698500758)
XLA Ops:
  0.0 37.6 %exchange.1 = (f32[16,8192]{1,0:T(8,128)}, bf16[16,8192]{1,0:T(8,128)(2,1)}, f32[256,8192]{1,0:T(8,128)}) custom-call(s32[4]{0:T(128)} %lengths_ref.3, bf16[3,256,8192]{2,1,0:T(8,128)(2,1)} %bitcast.3, f32[3,3,8192]{2,1,0:T(4,128)} %taps_ref.3, f32[16,8192]{1,0:T(8,128)} %rate_ref.1, f32[16,8192]{1,0:T(8,128)} %residue_ref.1, f32[1,8192]{1,0:T(1,128)} %bitcast.5, ...), custom_call_target="tpu_custom_call" | custom-call | tf_op jit(solution)/shard_map/exchange/pallas_call | solution.py:481
  37.6 12.1 %output.1 = (bf16[256,8192]{1,0:T(8,128)(2,1)}, f32[256,128]{1,0:T(8,128)}) custom-call(s32[4]{0:T(128)} %lengths_ref.3, bf16[3,256,8192]{2,1,0:T(8,128)(2,1)} %bitcast.4, f32[256,8192]{1,0:T(8,128)} %get-tuple-element.9.total_ref, bf16[16,8192]{1,0:T(8,128)(2,1)} %get-tuple-element.10.edge_ref, f32[3,3,8192]{2,1,0:T(4,128)} %taps_ref.3, f32[1,8192]{1,0:T(1,128)} %bitcast.6, ...), custom_call_target="tpu_custom_call" | custom-call | tf_op jit(solution)/shard_map/output/pallas_call | solution.py:547
